TPU v7x, 256 devices: a whole 4x4x8 slice. The times are simulated.
256 devices in a mesh: psi: 8 (over z), theta: 32 (over y, x, core).
Axes of the slice: x: 4, y: 4, z: 8, core: 2. Of those that a mesh axis runs over, the one named last changes fastest.
Arguments:
- sample_values: float32 [262144], P('theta'), may hold values from -6 to 6
- sample_coords: float32 [3, 262144], P(None, 'theta'), may hold values from 0 to 0.999
- tile_ids: int32 [262144, 1], P('theta'), may hold values from 0 to 31; in each aligned block of 8192 rows (0 to 8191, 8192 to 16383, ...) at most 512 rows name the same one
- phi_pixels: int32 [262144], P('theta'), may hold values from 0 to 2303
- wigner_table: bfloat16 [1152, 16, 32, 1152], P('theta', 'psi'), may hold values from -1 to 1
- beam: float32 [16, 1152], P('psi'), may hold values from -6 to 6
Outputs:
- sky: float32 [2, 1152, 1152], P(None, 'theta', 'psi')
Inputs may be any that keep to these rules, and one draw needn't show every extreme that they name: `tile_ids`: at most 512 of the samples of one device name the same cycle.
All inputs are finite; a program needn't handle non-finite values.
Results may differ from a plain program's by a relative error of at most 0.006.
Values may be sent and summed in bfloat16 or wider, within the bound.
No kernel may reach another device: no remote copies, remote signals or barrier semaphores. Data moves between devices by JAX's collectives and lax.ppermute only.
A program may use at most 128 MiB of HBM per device.

v0:
```python
import math

import jax
import jax.numpy as jnp
import numpy as np
from jax import lax
from jax.experimental import pallas as pl
from jax.experimental.pallas import tpu as pltpu
from jax.sharding import PartitionSpec as P

LANES = 128
STRIDE = 253
BLOCK = 256
NT = (((1,), (1,)), ((), ()))


def fourier_rows(nphi, blocks):
    pixel = (STRIDE * np.arange(blocks)[:, None] + np.arange(BLOCK)[None, :] - 1) % nphi
    waves = np.arange(nphi // 2)
    phase = (2.0 * math.pi / nphi) * (waves[:, None] * pixel.reshape(1, -1) % nphi)
    return np.stack([np.cos(phase), -np.sin(phase)]).astype(jnp.bfloat16)


def deposit_kernel(
    blocks, cycles, nphi, nyquist, psi_ref, v_ref, coords_ref, t_ref, o_ref, table_hbm, out_ref,
    fields, ids, left, right, cube, table, sem,
):
    copy = pltpu.make_async_copy(table_hbm, table, sem)
    copy.start()
    rows = v_ref.shape[0]
    for i in range(rows):
        for k in range(3):
            fields[k, i : i + 1, :] = coords_ref[k : k + 1, i * LANES : (i + 1) * LANES]
    group = psi_ref[0]
    cycle_frac, pixel_frac, turns = fields[0], fields[1], fields[2]
    value = v_ref[...]

    def angle(harmonic):
        phase = turns * harmonic.astype(jnp.float32)
        return (2.0 * math.pi) * (phase - jnp.round(phase))

    even = jnp.where(group == 0, 1.0, 2.0 * jnp.sin(angle(group))) * value
    odd = jnp.where(group == nyquist - 1, 1.0, 2.0) * jnp.cos(angle(group + 1)) * value
    pixel = o_ref[...]
    block = (pixel.astype(jnp.float32) * (1.0 / STRIDE) + 0.5 / STRIDE).astype(jnp.int32)
    fields[0] = even * (1.0 - cycle_frac)
    fields[3] = even * cycle_frac
    fields[4] = odd * (1.0 - cycle_frac)
    fields[5] = odd * cycle_frac
    fields[1] = 0.5 * ((pixel - STRIDE * block + 1).astype(jnp.float32) + pixel_frac)
    ids[...] = block
    cube[...] = jnp.zeros_like(cube)
    cycle_ids = lax.broadcasted_iota(jnp.int32, (cycles, LANES), 0)
    columns = 0.5 * lax.broadcasted_iota(jnp.int32, (BLOCK, LANES), 0).astype(jnp.float32)
    width = left.shape[1] // LANES

    def chunk(step, carry):
        for j in range(width):
            row = pl.ds(step * width + j, 1)
            lanes = slice(j * LANES, (j + 1) * LANES)
            cycle = t_ref[row, :]
            here, after = cycle_ids == cycle, cycle_ids == cycle + 1
            hats = [
                jnp.where(here, fields[a, row, :], jnp.where(after, fields[b, row, :], 0.0))
                for a, b in ((0, 3), (4, 5))
            ]
            own = ids[row, :]
            for b in range(blocks):
                mine = own == b
                for c in range(2):
                    start = (2 * b + c) * cycles
                    left[start : start + cycles, lanes] = jnp.where(mine, hats[c], 0.0).astype(
                        jnp.bfloat16
                    )
            offset = columns - fields[1, row, :]
            inner = jnp.maximum(1.0 - offset * offset, 0.0)
            right[:, lanes] = (inner * inner).astype(jnp.bfloat16)
        cube[...] += lax.dot_general(
            left[...], right[...], NT, preferred_element_type=jnp.float32
        )
        return carry

    lax.fori_loop(0, rows // width, chunk, 0)
    copy.wait()
    spread = jnp.concatenate(
        [cube[b * 2 * cycles : (b + 1) * 2 * cycles, :].astype(jnp.bfloat16) for b in range(blocks)],
        axis=1,
    )
    waves = [
        lax.dot_general(table[x], spread, NT, preferred_element_type=jnp.float32) for x in range(2)
    ]
    out_ref[...] = (jnp.concatenate(waves, axis=1) * (1.0 / math.sqrt(nphi))).astype(jnp.bfloat16)


def partial_orders(group, values, coords, cycle_ids, pixels, cycles, nphi, nyquist):
    blocks = -(-nphi // STRIDE)
    rows = values.shape[0] // LANES
    depth = blocks * BLOCK
    table = jnp.asarray(fourier_rows(nphi, blocks))
    chunk = 8 * LANES
    vmem = pl.BlockSpec(memory_space=pltpu.VMEM)
    return pl.pallas_call(
        lambda *refs: deposit_kernel(blocks, cycles, nphi, nyquist, *refs),
        out_shape=jax.ShapeDtypeStruct((nphi // 2, 4 * cycles), jnp.bfloat16),
        in_specs=[pl.BlockSpec(memory_space=pltpu.SMEM)] + [vmem] * 4 + [pl.BlockSpec(memory_space=pl.ANY)],
        out_specs=vmem,
        scratch_shapes=[
            pltpu.VMEM((6, rows, LANES), jnp.float32),
            pltpu.VMEM((rows, LANES), jnp.int32),
            pltpu.VMEM((2 * cycles * blocks, chunk), jnp.bfloat16),
            pltpu.VMEM((BLOCK, chunk), jnp.bfloat16),
            pltpu.VMEM((2 * cycles * blocks, BLOCK), jnp.float32),
            pltpu.VMEM((2, nphi // 2, depth), jnp.bfloat16),
            pltpu.SemaphoreType.DMA,
        ],
        compiler_params=pltpu.CompilerParams(vmem_limit_bytes=48 * 2**20),
    )(
        group,
        values.reshape(rows, LANES),
        coords,
        cycle_ids.reshape(rows, LANES),
        pixels.reshape(rows, LANES),
        table,
    )


def project_kernel(scale, parts_ref, wigner_ref, beam_ref, out_ref, total):
    senders, orders, lanes = parts_ref.shape
    depth = lanes // 2
    pack = BLOCK // depth
    groups = orders // pack
    waves = wigner_ref.shape[2]
    summed = jnp.sum(parts_ref[...].astype(jnp.float32), axis=0).astype(jnp.bfloat16)
    expand = (
        lax.broadcasted_iota(jnp.int32, (2 * orders, orders), 0) // 2
        == lax.broadcasted_iota(jnp.int32, (2 * orders, orders), 1)
    ).astype(jnp.bfloat16)
    tall = jnp.dot(expand, summed, preferred_element_type=jnp.float32)
    row = lax.broadcasted_iota(jnp.int32, (2 * orders, BLOCK), 0)
    lane = lax.broadcasted_iota(jnp.int32, (2 * orders, BLOCK), 1)
    keep = (row % (2 * pack)) == (lane // (depth // 2))
    lhs = [
        jnp.where(keep, jnp.concatenate([tall[:, x * depth : (x + 1) * depth]] * pack, axis=1), 0.0)
        for x in range(2)
    ]
    beam = beam_ref[...] * scale
    weight = jnp.concatenate([beam] * pack, axis=0)
    for g in range(groups):
        rows = slice(2 * pack * g, 2 * pack * (g + 1))
        both = jnp.concatenate([lhs[0][rows], lhs[1][rows]], axis=0).astype(jnp.bfloat16)
        product = jnp.dot(both, wigner_ref[g], preferred_element_type=jnp.float32)
        for x in range(2):
            part = product[x * 2 * pack : (x + 1) * 2 * pack] * weight
            total[x, rows, :] = part
    step = out_ref.shape[2]
    for x in range(2):
        sky = jnp.sum(total[x].reshape(orders, 2, waves), axis=1)
        for k in range(out_ref.shape[0]):
            out_ref[k, x * orders : (x + 1) * orders, :] = sky[:, k * step : (k + 1) * step].astype(
                jnp.bfloat16
            )


def partial_sky(parts, wigner, beam, groups, scale):
    orders, channels, cycles, waves = wigner.shape
    pack = BLOCK // (channels * cycles)
    vmem = pl.BlockSpec(memory_space=pltpu.VMEM)
    return pl.pallas_call(
        lambda *refs: project_kernel(scale, *refs),
        out_shape=jax.ShapeDtypeStruct((groups, 2 * orders, waves // groups), jnp.bfloat16),
        in_specs=[vmem] * 3,
        out_specs=vmem,
        scratch_shapes=[pltpu.VMEM((2, 2 * orders, waves), jnp.float32)],
        compiler_params=pltpu.CompilerParams(vmem_limit_bytes=48 * 2**20),
    )(parts, wigner.reshape(orders // pack, BLOCK, waves), beam)


def body(sample_values, sample_coords, tile_ids, phi_pixels, wigner_table, beam):
    tiles = lax.axis_size("theta")
    groups = lax.axis_size("psi")
    orders, channels, cycles, waves = wigner_table.shape
    nphi = 2 * tiles * orders
    nyquist = groups * channels // 2
    group = lax.axis_index("psi").astype(jnp.int32).reshape(1)
    freq = partial_orders(
        group, sample_values, sample_coords, tile_ids, phi_pixels, cycles, nphi, nyquist
    )
    freq = lax.all_to_all(
        freq.reshape(tiles, orders, freq.shape[1]), "theta", split_axis=0, concat_axis=0, tiled=True
    )
    sky = partial_sky(freq, wigner_table, beam, groups, 1.0 / math.sqrt(groups * channels))
    sky = lax.all_to_all(sky, "psi", split_axis=0, concat_axis=0, tiled=True)
    sky = jnp.sum(sky.astype(jnp.float32), axis=0)
    return sky.reshape(2, orders, waves // groups)


def solution(mesh):
    in_specs = (
        P("theta"),
        P(None, "theta"),
        P("theta", None),
        P("theta"),
        P("theta", "psi", None, None),
        P("psi", None),
    )
    out_specs = P(None, "theta", "psi")
    return jax.shard_map(body, mesh=mesh, in_specs=in_specs, out_specs=out_specs, check_vma=False)
```

profile of v0, /device:TPU:1, one launch (start us, length us, event | category | flops | bytes accessed | tf_op | source)
XLA Modules:
  0.0 56.9 jit_solution(4924194072136281489)
XLA Ops:
  0.0 0.0 copy-start.5
  0.0 0.0 copy-start.1
  0.0 0.9 %copy-done.1 = f32[3,8192]{1,0:T(4,128)S(1)} copy-done((f32[3,8192]{1,0:T(4,128)S(1)}, f32[3,8192]{1,0:T(4,128)}, u32[]{:S(2)}) %copy-start.1) | copy-done | bytes 98328
  0.9 0.0 copy-start.2
  0.9 0.8 %copy-done.2 = f32[8192]{0:T(1024)S(1)} copy-done((f32[8192]{0:T(1024)S(1)}, f32[8192]{0:T(1024)}, u32[]{:S(2)}) %copy-start.2) | copy-done | bytes 32792
  1.7 0.0 copy-start.3
  1.7 0.8 %copy-done.3 = s32[8192,1]{0,1:T(1,128)S(1)} copy-done((s32[8192,1]{0,1:T(1,128)S(1)}, s32[8192,1]{0,1:T(1,128)}, u32[]{:S(2)}) %copy-start.3) | copy-done | bytes 32792
  2.4 0.0 copy-start.4
  2.4 0.8 %copy-done.4 = s32[8192]{0:T(1024)S(1)} copy-done((s32[8192]{0:T(1024)S(1)}, s32[8192]{0:T(1024)}, u32[]{:S(2)}) %copy-start.4) | copy-done | bytes 32792
  3.2 10.7 %shard_map.73 = bf16[1152,128]{1,0:T(8,128)(2,1)S(1)} custom-call(s32[1]{0:T(128)} %bitcast.refs_0_, f32[64,128]{1,0:T(8,128)S(1)} %bitcast.6, f32[3,8192]{1,0:T(4,128)S(1)} %copy-done.1, s32[64,128]{1,0:T(8,128)S(1)} %bitcast.7, s32[64,128]{1,0:T(8,128)S(1)} %bitcast.8, bf16[2,1152,2560]{2,1,0:T(8,128)(2,1)} %constant.10.clone.refs_5_), custom_call_target="tpu_custom_call" | custom-call | tf_op jit(solution)/shard_map/pallas_call | solution.py:102
  13.9 0.1 reshape.25
  13.9 17.9 %all_to_all.10.refs_0_ = bf16[32,36,128]{2,1,0:T(8,128)(2,1)S(1)} all-to-all(bf16[32,36,128]{2,1,0:T(8,128)(2,1)S(1)} %reshape.25), channel_id=1, replica_groups=mesh['psi'=8,'theta'=32] {'theta'}, dimensions={0} | all-to-all | bytes 589824 | tf_op jit(solution)/shard_map/all_to_all | solution.py:188
  31.9 0.0 copy-done.5
  31.9 0.0 copy-start
  31.9 2.5 %copy-done = bf16[36,2,32,1152]{3,2,1,0:T(8,128)(2,1)S(1)} copy-done((bf16[36,2,32,1152]{3,2,1,0:T(8,128)(2,1)S(1)}, bf16[36,2,32,1152]{3,2,1,0:T(8,128)(2,1)}, u32[]{:S(2)}) %copy-start) | copy-done | bytes 5308440
  34.4 1.5 %shard_map.74 = bf16[8,72,144]{2,1,0:T(8,128)(2,1)S(1)} custom-call(bf16[32,36,128]{2,1,0:T(8,128)(2,1)S(1)} %all_to_all.10.refs_0_, bf16[9,256,1152]{2,1,0:T(8,128)(2,1)S(1)} %bitcast.5, f32[2,1152]{1,0:T(2,128)S(1)} %copy-done.5), custom_call_target="tpu_custom_call" | custom-call | tf_op jit(solution)/shard_map/pallas_call | solution.py:168
  35.9 20.3 %all_to_all.11 = bf16[8,72,144]{2,1,0:T(8,128)(2,1)S(1)} all-to-all(bf16[8,72,144]{2,1,0:T(8,128)(2,1)S(1)} %shard_map.74), channel_id=1, replica_groups=mesh['psi'=8,'theta'=32] {'psi'}, dimensions={0} | all-to-all | bytes 331776 | tf_op jit(solution)/shard_map/all_to_all | solution.py:192
  56.2 0.1 convert_reduce_fusion
  56.3 0.7 %copy.8 = f32[2,36,144]{2,0,1:T(2,128)} copy(f32[2,36,144]{2,1,0:T(8,128)S(1)} %reshape.27) | data formatting | bytes 82944 | tf_op jit(solution)/shard_map/reshape | solution.py:194
  (1 shorter events, 0.0 us)
Async XLA Ops:
  0.0 31.9 %copy-start.5 = (f32[2,1152]{1,0:T(2,128)S(1)}, f32[2,1152]{1,0:T(2,128)}, u32[]{:S(2)}) copy-start(f32[2,1152]{1,0:T(2,128)} %refs_2_.3) | copy-start | bytes 27652
  0.0 0.9 %copy-start.1 = (f32[3,8192]{1,0:T(4,128)S(1)}, f32[3,8192]{1,0:T(4,128)}, u32[]{:S(2)}) copy-start(f32[3,8192]{1,0:T(4,128)} %refs_2_.2) | copy-start | bytes 294916
  0.9 0.8 %copy-start.2 = (f32[8192]{0:T(1024)S(1)}, f32[8192]{0:T(1024)}, u32[]{:S(2)}) copy-start(f32[8192]{0:T(1024)} %param.7) | copy-start | bytes 98308
  1.7 0.8 %copy-start.3 = (s32[8192,1]{0,1:T(1,128)S(1)}, s32[8192,1]{0,1:T(1,128)}, u32[]{:S(2)}) copy-start(s32[8192,1]{0,1:T(1,128)} %param.9) | copy-start | bytes 98308
  2.4 0.8 %copy-start.4 = (s32[8192]{0:T(1024)S(1)}, s32[8192]{0:T(1024)}, u32[]{:S(2)}) copy-start(s32[8192]{0:T(1024)} %param.10) | copy-start | bytes 98308
  31.9 2.5 %copy-start = (bf16[36,2,32,1152]{3,2,1,0:T(8,128)(2,1)S(1)}, bf16[36,2,32,1152]{3,2,1,0:T(8,128)(2,1)}, u32[]{:S(2)}) copy-start(bf16[36,2,32,1152]{3,2,1,0:T(8,128)(2,1)} %param.11) | copy-start | bytes 15925252
where the time goes:
time: 57.3 us; the launch traced here: 56.9 us
  blocking collectives  38.2 us (67%)
  Pallas kernels  12.2 us (21%)
  local copies, waits for them, and re-layouts  6.44 us (11%)
    all_to_all x1, blocking collectives, body(): sky = lax.all_to_all(sky, 'psi', split_axis=0, concat_axis=0, tiled=True)  20.3 us
    all_to_all x1, blocking collectives, body(): lax.all_to_all(freq.reshape(tiles, orders, freq.shape[1]), 'theta', split...  17.9 us
    pallas_call x1, Pallas kernels, partial_orders(): pl.pallas_call(lambda *refs: deposit_kernel(blocks, cycles, nphi, nyquist...  10.7 us
    unnamed x12, local copies, waits for them, and re-layouts  5.7 us
    pallas_call x1, Pallas kernels, partial_sky(): pl.pallas_call(lambda *refs: project_kernel(scale, *refs), out_shape=jax....  1.51 us

commit v1 on v0

v1 whole, which is shorter than its diff:
```python
import math

import jax
import jax.numpy as jnp
import numpy as np
from jax import lax
from jax.experimental import pallas as pl
from jax.experimental.pallas import tpu as pltpu
from jax.sharding import PartitionSpec as P

LANES = 128
STRIDE = 253
BLOCK = 256
RADIX = 9
NT = (((1,), (1,)), ((), ()))


def fourier_rows(nphi):
    waves = np.arange(nphi // 2).reshape(-1, RADIX).T
    phase = (2.0 * math.pi / nphi) * (waves[:, :, None] * (np.arange(BLOCK) - 1) % nphi)
    return np.concatenate([np.cos(phase), np.sin(phase)], axis=2)


def phase_sums(runs):
    half = RADIX // 2
    even = [runs[b] + runs[RADIX - b] for b in range(1, half + 1)]
    odd = [runs[b] - runs[RADIX - b] for b in range(1, half + 1)]
    sums = []
    for k in range(half + 1):
        real, imag = runs[0], None
        for b in range(1, half + 1):
            turn = 2.0 * math.pi * (k * b % RADIX) / RADIX
            real = real + (even[b - 1] if k == 0 else math.cos(turn) * even[b - 1])
            if k:
                part = -math.sin(turn) * odd[b - 1]
                imag = part if imag is None else imag + part
        sums.append((real, imag))
    return sums


def split(x):
    high = x.astype(jnp.bfloat16)
    return high, (x - high.astype(jnp.float32)).astype(jnp.bfloat16)


def deposit_kernel(
    blocks, cycles, nphi, nyquist, psi_ref, v_hbm, coords_hbm, t_hbm, o_hbm, table_hbm, out_ref,
    values, coords, cycle_of, pixels, fields, left, right, cube, table, spread, sems,
):
    sources = (v_hbm, coords_hbm, o_hbm, t_hbm, table_hbm)
    targets = (values, coords, pixels, cycle_of, table)
    copies = [
        pltpu.make_async_copy(source, target, sems.at[i])
        for i, (source, target) in enumerate(zip(sources, targets))
    ]
    for copy in copies:
        copy.start()
    cube[...] = jnp.zeros_like(cube)
    group = psi_ref[0]
    for copy in copies[:3]:
        copy.wait()
    rows = values.shape[0]
    for i in range(rows):
        for k in range(3):
            fields[k, i : i + 1, :] = coords[k : k + 1, i * LANES : (i + 1) * LANES]
    cycle_frac, pixel_frac, turns = fields[0], fields[1], fields[2]
    value = values[...]

    def angle(harmonic):
        phase = turns * harmonic.astype(jnp.float32)
        return (2.0 * math.pi) * (phase - jnp.round(phase))

    even = jnp.where(group == 0, 1.0, 2.0 * jnp.sin(angle(group))) * value
    odd = jnp.where(group == nyquist - 1, 1.0, 2.0) * jnp.cos(angle(group + 1)) * value
    pixel = pixels[...]
    block = (pixel.astype(jnp.float32) * (1.0 / STRIDE) + 0.5 / STRIDE).astype(jnp.int32)
    fields[0] = even * (1.0 - cycle_frac)
    fields[3] = even * cycle_frac
    fields[4] = odd * (1.0 - cycle_frac)
    fields[5] = odd * cycle_frac
    fields[1] = 0.5 * ((pixel - STRIDE * block + 1).astype(jnp.float32) + pixel_frac)
    pixels[...] = block
    copies[3].wait()
    cycle_ids = lax.broadcasted_iota(jnp.int32, (cycles, LANES), 0)
    columns = 0.5 * lax.broadcasted_iota(jnp.int32, (BLOCK, LANES), 0).astype(jnp.float32)
    width = left.shape[1] // LANES

    def chunk(step, carry):
        for j in range(width):
            row = pl.ds(step * width + j, 1)
            lanes = slice(j * LANES, (j + 1) * LANES)
            cycle = cycle_of[row, :]
            here, after = cycle_ids == cycle, cycle_ids == cycle + 1
            hats = [
                jnp.where(here, fields[a, row, :], jnp.where(after, fields[b, row, :], 0.0))
                for a, b in ((0, 3), (4, 5))
            ]
            own = pixels[row, :]
            for b in range(blocks):
                mine = own == b
                for c in range(2):
                    start = (2 * b + c) * cycles
                    left[start : start + cycles, lanes] = jnp.where(mine, hats[c], 0.0).astype(
                        jnp.bfloat16
                    )
            offset = columns - fields[1, row, :]
            inner = jnp.maximum(1.0 - offset * offset, 0.0)
            right[:, lanes] = (inner * inner).astype(jnp.bfloat16)
        cube[...] += lax.dot_general(
            left[...], right[...], NT, preferred_element_type=jnp.float32
        )
        return carry

    lax.fori_loop(0, rows // width, chunk, 0)
    lines = 2 * cycles
    tiles = nphi // LANES
    sums = [None] * tiles
    blank = jnp.zeros((lines, LANES), jnp.float32)
    for b in range(blocks):
        first, shift = divmod(b * STRIDE, LANES)
        block_rows = cube[b * lines : (b + 1) * lines, :]
        wide = jnp.concatenate([block_rows, blank], axis=1)
        if shift:
            wide = pltpu.roll(wide, shift, 1)
        for k in range(3):
            part = wide[:, k * LANES : (k + 1) * LANES]
            tile = (first + k) % tiles
            sums[tile] = part if sums[tile] is None else sums[tile] + part
    per_run = BLOCK // LANES
    runs = [jnp.concatenate(sums[b * per_run : (b + 1) * per_run], axis=1) for b in range(RADIX)]
    groups = phase_sums(runs)
    copies[4].wait()
    share = out_ref.shape[1] // RADIX
    for m in range(RADIX):
        real, imag = groups[min(m, RADIX - m)]
        imag = jnp.zeros_like(real) if m == 0 else (imag if m <= RADIX // 2 else -imag)
        operand = jnp.concatenate(
            [jnp.concatenate([real, imag], axis=1), jnp.concatenate([imag, -real], axis=1)], axis=0
        ) * (1.0 / math.sqrt(nphi))
        waves = sum(
            lax.dot_general(table[m], part, NT, preferred_element_type=jnp.float32)
            for part in split(operand)
        )
        for d in range(out_ref.shape[0]):
            spread[d, m * share : (m + 1) * share, :] = waves[d * share : (d + 1) * share]
    out_ref[...] = spread[...].astype(jnp.bfloat16)


def partial_orders(group, values, coords, cycle_ids, pixels, cycles, nphi, nyquist, tiles=32):
    blocks = -(-nphi // STRIDE)
    rows = values.shape[0] // LANES
    table = jnp.asarray(fourier_rows(nphi).astype(jnp.bfloat16))
    chunk = 8 * LANES
    vmem = pl.BlockSpec(memory_space=pltpu.VMEM)
    whole = (tiles, nphi // 2 // tiles, 4 * cycles)
    return pl.pallas_call(
        lambda *refs: deposit_kernel(blocks, cycles, nphi, nyquist, *refs),
        out_shape=jax.ShapeDtypeStruct(whole, jnp.bfloat16),
        in_specs=[pl.BlockSpec(memory_space=pltpu.SMEM)] + [pl.BlockSpec(memory_space=pltpu.HBM)] * 5,
        out_specs=vmem,
        scratch_shapes=[
            pltpu.VMEM((rows, LANES), jnp.float32),
            pltpu.VMEM(coords.shape, jnp.float32),
            pltpu.VMEM((rows, LANES), jnp.int32),
            pltpu.VMEM((rows, LANES), jnp.int32),
            pltpu.VMEM((6, rows, LANES), jnp.float32),
            pltpu.VMEM((2 * cycles * blocks, chunk), jnp.bfloat16),
            pltpu.VMEM((BLOCK, chunk), jnp.bfloat16),
            pltpu.VMEM((2 * cycles * blocks, BLOCK), jnp.float32),
            pltpu.VMEM(table.shape, jnp.bfloat16),
            pltpu.VMEM(whole, jnp.float32),
            pltpu.SemaphoreType.DMA((5,)),
        ],
        compiler_params=pltpu.CompilerParams(vmem_limit_bytes=24 * 2**20),
    )(
        group,
        values.reshape(rows, LANES),
        coords,
        cycle_ids.reshape(rows, LANES),
        pixels.reshape(rows, LANES),
        table,
    )


def project_kernel(scale, parts_ref, wigner_ref, beam_ref, out_ref, sky):
    orders, lanes = parts_ref.shape[1:]
    depth = lanes // 2
    pack = BLOCK // depth
    summed = split(jnp.sum(parts_ref[...].astype(jnp.float32), axis=0))
    row = lax.broadcasted_iota(jnp.int32, (2 * orders, orders), 0)
    place = lax.broadcasted_iota(jnp.int32, (2 * orders, orders), 1)
    order = row // 2
    found = (order % RADIX) * (orders // RADIX) + order // RADIX == place
    chosen = [(found & (row % 2 == x)).astype(jnp.bfloat16) for x in range(2)]
    row = lax.broadcasted_iota(jnp.int32, (2 * orders, BLOCK), 0)
    lane = lax.broadcasted_iota(jnp.int32, (2 * orders, BLOCK), 1)
    mine = row // 2 % pack == lane // depth
    second = lane // (depth // 2) % 2
    tops = []
    for part in summed:
        tall = sum(
            jnp.dot(chosen[x], part[:, x * depth : (x + 1) * depth], preferred_element_type=jnp.float32)
            for x in range(2)
        )
        wide = jnp.concatenate([tall] * pack, axis=1)
        tops += [jnp.where(mine & (second == c), wide, 0.0) for c in range(2)]
    beam = beam_ref[...] * scale
    height = 2 * pack
    for g in range(orders // pack):
        rows = slice(height * g, height * (g + 1))
        lhs = jnp.concatenate([top[rows] for top in tops], axis=0).astype(jnp.bfloat16)
        product = jnp.dot(lhs, wigner_ref[g], preferred_element_type=jnp.float32)
        first, other = (
            product[c * height : (c + 1) * height] + product[(c + 2) * height : (c + 3) * height]
            for c in range(2)
        )
        sky[rows, :] = first * beam[0:1] + other * beam[1:2]
    step = sky.shape[1] // out_ref.shape[0]
    over = step - LANES
    fold = LANES // over
    piece = sky.shape[0] // fold
    for k in range(out_ref.shape[0]):
        start = k * step
        rest = [
            sky[j * piece : (j + 1) * piece, start + LANES : start + step] for j in range(fold)
        ]
        out_ref[k] = jnp.concatenate(
            [sky[:, start : start + LANES], jnp.concatenate(rest, axis=1)], axis=0
        ).astype(jnp.bfloat16)


def partial_sky(parts, wigner, beam, groups, scale):
    orders, channels, cycles, waves = wigner.shape
    pack = BLOCK // (channels * cycles)
    vmem = pl.BlockSpec(memory_space=pltpu.VMEM)
    whole = (groups, 2 * orders * (waves // groups) // LANES, LANES)
    return pl.pallas_call(
        lambda *refs: project_kernel(scale, *refs),
        out_shape=jax.ShapeDtypeStruct(whole, jnp.bfloat16),
        in_specs=[vmem] * 3,
        out_specs=vmem,
        scratch_shapes=[pltpu.VMEM((2 * orders, waves), jnp.float32)],
        compiler_params=pltpu.CompilerParams(vmem_limit_bytes=24 * 2**20),
    )(parts, wigner.reshape(orders // pack, BLOCK, waves), beam)


def finish_kernel(parts_ref, out_ref):
    total = jnp.sum(parts_ref[...].astype(jnp.float32), axis=0)
    orders, two, waves = out_ref.shape
    over = waves - LANES
    fold = LANES // over
    main, rest = total[: 2 * orders], total[2 * orders :]
    tail = jnp.concatenate([rest[:, j * over : (j + 1) * over] for j in range(fold)], axis=0)
    out_ref[...] = jnp.concatenate([main, tail], axis=1).reshape(orders, two, waves)


def finish(parts, orders, waves):
    vmem = pl.BlockSpec(memory_space=pltpu.VMEM)
    return pl.pallas_call(
        finish_kernel,
        out_shape=jax.ShapeDtypeStruct((orders, 2, waves), jnp.float32),
        in_specs=[vmem],
        out_specs=vmem,
    )(parts)


def body(sample_values, sample_coords, tile_ids, phi_pixels, wigner_table, beam):
    tiles = lax.axis_size("theta")
    groups = lax.axis_size("psi")
    orders, channels, cycles, waves = wigner_table.shape
    nphi = 2 * tiles * orders
    nyquist = groups * channels // 2
    group = lax.axis_index("psi").astype(jnp.int32).reshape(1)
    freq = partial_orders(
        group, sample_values, sample_coords, tile_ids, phi_pixels, cycles, nphi, nyquist, tiles
    )
    freq = lax.all_to_all(freq, "theta", split_axis=0, concat_axis=0, tiled=True)
    sky = partial_sky(freq, wigner_table, beam, groups, 1.0 / math.sqrt(groups * channels))
    sky = lax.all_to_all(sky, "psi", split_axis=0, concat_axis=0, tiled=True)
    return jnp.moveaxis(finish(sky, orders, waves // groups), 1, 0)


def solution(mesh):
    in_specs = (
        P("theta"),
        P(None, "theta"),
        P("theta", None),
        P("theta"),
        P("theta", "psi", None, None),
        P("psi", None),
    )
    out_specs = P(None, "theta", "psi")
    return jax.shard_map(body, mesh=mesh, in_specs=in_specs, out_specs=out_specs, check_vma=False)
```

time: 57.3 us -> 55.6 us (0.970)
  the two profiles are of different devices: /device:TPU:1 before, /device:TPU:2 now
where the time goes in v1:
time: 55.6 us; the launch traced here: 54.8 us
  blocking collectives  34.9 us (63%)
  Pallas kernels  12.2 us (22%)
  local copies, waits for them, and re-layouts  7.65 us (14%)
    all_to_all x1, blocking collectives, body(): sky = lax.all_to_all(sky, 'psi', split_axis=0, concat_axis=0, tiled=True)  19.1 us
    all_to_all x1, blocking collectives, body(): lax.all_to_all(freq, 'theta', split_axis=0, concat_axis=0, tiled=True)  15.8 us
    pallas_call x1, Pallas kernels, partial_orders(): pl.pallas_call(lambda *refs: deposit_kernel(blocks, cycles, nphi, nyquist...  9.14 us
    unnamed x14, local copies, waits for them, and re-layouts  7.65 us
    pallas_call x1, Pallas kernels, finish(): pl.pallas_call(finish_kernel, out_shape=jax.ShapeDtypeStruct((orders, 2,...  1.65 us
    pallas_call x1, Pallas kernels, partial_sky(): pl.pallas_call(lambda *refs: project_kernel(scale, *refs), out_shape=jax....  1.43 us

profile of v1, /device:TPU:2, one launch (start us, length us, event | category | flops | bytes accessed | tf_op | source)
XLA Modules:
  0.0 54.8 jit_solution(7429106087702406109)
XLA Ops:
  0.0 0.0 copy-start.1
  0.0 1.3 %copy-done.1 = bf16[9,128,512]{2,1,0:T(8,128)(2,1)S(1)} copy-done((bf16[9,128,512]{2,1,0:T(8,128)(2,1)S(1)}, bf16[9,128,512]{2,1,0:T(8,128)(2,1)}, u32[]{:S(2)}) %copy-start.1) | copy-done | bytes 1179672
  1.3 0.0 copy-start.2
  1.3 0.9 %copy-done.2 = f32[3,8192]{1,0:T(4,128)S(1)} copy-done((f32[3,8192]{1,0:T(4,128)S(1)}, f32[3,8192]{1,0:T(4,128)}, u32[]{:S(2)}) %copy-start.2) | copy-done | bytes 98328
  2.2 0.0 copy-start.3
  2.2 0.8 %copy-done.3 = f32[8192]{0:T(1024)S(1)} copy-done((f32[8192]{0:T(1024)S(1)}, f32[8192]{0:T(1024)}, u32[]{:S(2)}) %copy-start.3) | copy-done | bytes 32792
  2.9 0.0 copy-start.4
  2.9 0.8 %copy-done.4 = s32[8192,1]{0,1:T(1,128)S(1)} copy-done((s32[8192,1]{0,1:T(1,128)S(1)}, s32[8192,1]{0,1:T(1,128)}, u32[]{:S(2)}) %copy-start.4) | copy-done | bytes 32792
  3.7 0.0 copy-start.5
  3.7 0.8 %copy-done.5 = s32[8192]{0:T(1024)S(1)} copy-done((s32[8192]{0:T(1024)S(1)}, s32[8192]{0:T(1024)}, u32[]{:S(2)}) %copy-start.5) | copy-done | bytes 32792
  4.5 9.1 %shard_map.73 = bf16[32,36,128]{2,1,0:T(8,128)(2,1)S(1)} custom-call(s32[1]{0:T(128)} %bitcast.refs_0_, f32[64,128]{1,0:T(8,128)S(1)} %bitcast.7, f32[3,8192]{1,0:T(4,128)S(1)} %copy-done.2, s32[64,128]{1,0:T(8,128)S(1)} %bitcast.8, s32[64,128]{1,0:T(8,128)S(1)} %bitcast.9, bf16[9,128,512]{2,1,0:T(8,128)(2,1)S(1)} %copy-done.1), custom_call_target="tpu_custom_call" | custom-call | tf_op jit(solution)/shard_map/pallas_call | solution.py:156
  13.6 15.8 %all_to_all.10.refs_0_ = bf16[32,36,128]{2,1,0:T(8,128)(2,1)S(1)} all-to-all(bf16[32,36,128]{2,1,0:T(8,128)(2,1)S(1)} %shard_map.73), channel_id=1, replica_groups=mesh['psi'=8,'theta'=32] {'theta'}, dimensions={0} | all-to-all | bytes 589824 | tf_op jit(solution)/shard_map/all_to_all | solution.py:277
  29.4 0.0 copy-start
  29.4 2.5 %copy-done = bf16[36,2,32,1152]{3,2,1,0:T(8,128)(2,1)S(1)} copy-done((bf16[36,2,32,1152]{3,2,1,0:T(8,128)(2,1)S(1)}, bf16[36,2,32,1152]{3,2,1,0:T(8,128)(2,1)}, u32[]{:S(2)}) %copy-start) | copy-done | bytes 5308440
  31.9 0.0 copy-start.6
  31.9 0.7 %copy-done.6 = f32[2,1152]{1,0:T(2,128)S(1)} copy-done((f32[2,1152]{1,0:T(2,128)S(1)}, f32[2,1152]{1,0:T(2,128)}, u32[]{:S(2)}) %copy-start.6) | copy-done | bytes 9240
  32.6 1.4 %shard_map.74 = bf16[8,81,128]{2,1,0:T(8,128)(2,1)S(1)} custom-call(bf16[32,36,128]{2,1,0:T(8,128)(2,1)S(1)} %all_to_all.10.refs_0_, bf16[9,256,1152]{2,1,0:T(8,128)(2,1)S(1)} %bitcast.6, f32[2,1152]{1,0:T(2,128)S(1)} %copy-done.6), custom_call_target="tpu_custom_call" | custom-call | tf_op jit(solution)/shard_map/pallas_call | solution.py:237
  34.1 19.1 %all_to_all.11.parts_ref = bf16[8,81,128]{2,1,0:T(8,128)(2,1)} all-to-all(bf16[8,81,128]{2,1,0:T(8,128)(2,1)S(1)} %shard_map.74), channel_id=1, replica_groups=mesh['psi'=8,'theta'=32] {'psi'}, dimensions={0} | all-to-all | bytes 331776 | tf_op jit(solution)/shard_map/all_to_all | solution.py:279
  53.2 1.6 %shard_map.75 = f32[36,2,144]{2,1,0:T(2,128)} custom-call(bf16[8,81,128]{2,1,0:T(8,128)(2,1)} %all_to_all.11.parts_ref), custom_call_target="tpu_custom_call" | custom-call | tf_op jit(solution)/shard_map/pallas_call | solution.py:259
Async XLA Ops:
  0.0 1.3 %copy-start.1 = (bf16[9,128,512]{2,1,0:T(8,128)(2,1)S(1)}, bf16[9,128,512]{2,1,0:T(8,128)(2,1)}, u32[]{:S(2)}) copy-start(bf16[9,128,512]{2,1,0:T(8,128)(2,1)} %constant.8.clone.refs_5_) | copy-start | bytes 3538948
  1.3 0.9 %copy-start.2 = (f32[3,8192]{1,0:T(4,128)S(1)}, f32[3,8192]{1,0:T(4,128)}, u32[]{:S(2)}) copy-start(f32[3,8192]{1,0:T(4,128)} %refs_2_.2) | copy-start | bytes 294916
  2.2 0.8 %copy-start.3 = (f32[8192]{0:T(1024)S(1)}, f32[8192]{0:T(1024)}, u32[]{:S(2)}) copy-start(f32[8192]{0:T(1024)} %param.7) | copy-start | bytes 98308
  2.9 0.8 %copy-start.4 = (s32[8192,1]{0,1:T(1,128)S(1)}, s32[8192,1]{0,1:T(1,128)}, u32[]{:S(2)}) copy-start(s32[8192,1]{0,1:T(1,128)} %param.9) | copy-start | bytes 98308
  3.7 0.8 %copy-start.5 = (s32[8192]{0:T(1024)S(1)}, s32[8192]{0:T(1024)}, u32[]{:S(2)}) copy-start(s32[8192]{0:T(1024)} %param.10) | copy-start | bytes 98308
  29.4 2.5 %copy-start = (bf16[36,2,32,1152]{3,2,1,0:T(8,128)(2,1)S(1)}, bf16[36,2,32,1152]{3,2,1,0:T(8,128)(2,1)}, u32[]{:S(2)}) copy-start(bf16[36,2,32,1152]{3,2,1,0:T(8,128)(2,1)} %param.11) | copy-start | bytes 15925252
  31.9 0.7 %copy-start.6 = (f32[2,1152]{1,0:T(2,128)S(1)}, f32[2,1152]{1,0:T(2,128)}, u32[]{:S(2)}) copy-start(f32[2,1152]{1,0:T(2,128)} %refs_2_.3) | copy-start | bytes 27652

commit v2 on v1

--- a/solution.py
+++ b/solution.py
@@ -9,9 +9,13 @@
 from jax.sharding import PartitionSpec as P
 
 LANES = 128
-STRIDE = 253
+CELL = 32
+OWNED = CELL - 3
 BLOCK = 256
+CELLS = BLOCK // CELL
+STRIDE = OWNED * CELLS
 RADIX = 9
+CHUNK = 1024
 NT = (((1,), (1,)), ((), ()))
 
 
@@ -44,11 +48,12 @@
 
 
 def deposit_kernel(
-    blocks, cycles, nphi, nyquist, psi_ref, v_hbm, coords_hbm, t_hbm, o_hbm, table_hbm, out_ref,
-    values, coords, cycle_of, pixels, fields, left, right, cube, table, spread, sems,
+    blocks, cycles, nphi, nyquist, psi_ref, v_hbm, coords_hbm, t_hbm, o_hbm, table_hbm, wigner_hbm,
+    beam_hbm, out_ref, wigner, beam, values, coords, cycle_of, pixels, fields, left, right, cube,
+    table, spread, sems,
 ):
-    sources = (v_hbm, coords_hbm, o_hbm, t_hbm, table_hbm)
-    targets = (values, coords, pixels, cycle_of, table)
+    sources = (v_hbm, coords_hbm, o_hbm, t_hbm, table_hbm, beam_hbm, wigner_hbm)
+    targets = (values, coords, pixels, cycle_of, table, beam, wigner)
     copies = [
         pltpu.make_async_copy(source, target, sems.at[i])
         for i, (source, target) in enumerate(zip(sources, targets))
@@ -73,19 +78,20 @@
     even = jnp.where(group == 0, 1.0, 2.0 * jnp.sin(angle(group))) * value
     odd = jnp.where(group == nyquist - 1, 1.0, 2.0) * jnp.cos(angle(group + 1)) * value
     pixel = pixels[...]
-    block = (pixel.astype(jnp.float32) * (1.0 / STRIDE) + 0.5 / STRIDE).astype(jnp.int32)
+    cell = (pixel.astype(jnp.float32) * (1.0 / OWNED) + 0.5 / OWNED).astype(jnp.int32)
     fields[0] = even * (1.0 - cycle_frac)
     fields[3] = even * cycle_frac
     fields[4] = odd * (1.0 - cycle_frac)
     fields[5] = odd * cycle_frac
-    fields[1] = 0.5 * ((pixel - STRIDE * block + 1).astype(jnp.float32) + pixel_frac)
-    pixels[...] = block
+    fields[1] = 0.5 * ((pixel - OWNED * cell + 1).astype(jnp.float32) + pixel_frac)
+    fields[2] = (cell // CELLS).astype(jnp.float32)
+    fields[6] = (cell % CELLS).astype(jnp.float32)
     copies[3].wait()
     cycle_ids = lax.broadcasted_iota(jnp.int32, (cycles, LANES), 0)
-    columns = 0.5 * lax.broadcasted_iota(jnp.int32, (BLOCK, LANES), 0).astype(jnp.float32)
-    width = left.shape[1] // LANES
-
-    def chunk(step, carry):
+    columns = 0.5 * lax.broadcasted_iota(jnp.int32, (CELL, LANES), 0).astype(jnp.float32)
+    width = left.shape[2] // LANES
+
+    def fill(step, slot):
         for j in range(width):
             row = pl.ds(step * width + j, 1)
             lanes = slice(j * LANES, (j + 1) * LANES)
@@ -95,23 +101,46 @@
                 jnp.where(here, fields[a, row, :], jnp.where(after, fields[b, row, :], 0.0))
                 for a, b in ((0, 3), (4, 5))
             ]
-            own = pixels[row, :]
+            own, within = (
+                jnp.broadcast_to(fields[k, row, :], (CELL, LANES)).astype(jnp.bfloat16)
+                for k in (2, 6)
+            )
+            hats = [hat.astype(jnp.bfloat16) for hat in hats]
             for b in range(blocks):
-                mine = own == b
+                mine = own == jnp.bfloat16(b)
                 for c in range(2):
                     start = (2 * b + c) * cycles
-                    left[start : start + cycles, lanes] = jnp.where(mine, hats[c], 0.0).astype(
-                        jnp.bfloat16
-                    )
+                    left[slot, start : start + cycles, lanes] = jnp.where(mine, hats[c], jnp.bfloat16(0))
             offset = columns - fields[1, row, :]
             inner = jnp.maximum(1.0 - offset * offset, 0.0)
-            right[:, lanes] = (inner * inner).astype(jnp.bfloat16)
+            taps = (inner * inner).astype(jnp.bfloat16)
+            for q in range(CELLS):
+                right[slot, q * CELL : (q + 1) * CELL, lanes] = jnp.where(
+                    within == jnp.bfloat16(q), taps, jnp.bfloat16(0)
+                )
+
+    def add(slot):
         cube[...] += lax.dot_general(
-            left[...], right[...], NT, preferred_element_type=jnp.float32
+            left[slot], right[slot], NT, preferred_element_type=jnp.float32
         )
+
+    steps = rows // width
+    fill(0, 0)
+
+    def pair(step, carry):
+        fill(2 * step + 1, 1)
+        add(0)
+        fill(jnp.minimum(2 * step + 2, steps - 1), 0)
+        add(1)
         return carry
 
-    lax.fori_loop(0, rows // width, chunk, 0)
+    lax.fori_loop(0, steps // 2, pair, 0)
+    source = lax.broadcasted_iota(jnp.int32, (BLOCK, BLOCK), 0)
+    target = lax.broadcasted_iota(jnp.int32, (BLOCK, BLOCK), 1)
+    join = (source - 3 * (source // CELL) == target).astype(jnp.bfloat16)
+    cube[...] = sum(
+        jnp.dot(part, join, preferred_element_type=jnp.float32) for part in split(cube[...])
+    )
     lines = 2 * cycles
     tiles = nphi // LANES
     sums = [None] * tiles
@@ -137,49 +166,60 @@
         operand = jnp.concatenate(
             [jnp.concatenate([real, imag], axis=1), jnp.concatenate([imag, -real], axis=1)], axis=0
         ) * (1.0 / math.sqrt(nphi))
+        waves_m = table[m].astype(jnp.bfloat16)
         waves = sum(
-            lax.dot_general(table[m], part, NT, preferred_element_type=jnp.float32)
+            lax.dot_general(waves_m, part, NT, preferred_element_type=jnp.float32)
             for part in split(operand)
         )
         for d in range(out_ref.shape[0]):
             spread[d, m * share : (m + 1) * share, :] = waves[d * share : (d + 1) * share]
     out_ref[...] = spread[...].astype(jnp.bfloat16)
-
-
-def partial_orders(group, values, coords, cycle_ids, pixels, cycles, nphi, nyquist, tiles=32):
+    for copy in copies[5:]:
+        copy.wait()
+
+
+def partial_orders(group, values, coords, cycle_ids, pixels, wigner, beam, nphi, nyquist, tiles):
+    orders, channels, cycles, waves = wigner.shape
     blocks = -(-nphi // STRIDE)
     rows = values.shape[0] // LANES
-    table = jnp.asarray(fourier_rows(nphi).astype(jnp.bfloat16))
-    chunk = 8 * LANES
+    table = jnp.asarray(fourier_rows(nphi).astype(np.float32))
     vmem = pl.BlockSpec(memory_space=pltpu.VMEM)
-    whole = (tiles, nphi // 2 // tiles, 4 * cycles)
+    whole = (tiles, orders, 2 * channels * cycles)
+    wigner = wigner.reshape(orders * channels * cycles // BLOCK, BLOCK, waves)
+    operands = (
+        values.reshape(rows, LANES),
+        coords,
+        cycle_ids.reshape(rows, LANES),
+        pixels.reshape(rows, LANES),
+        table,
+        wigner,
+        beam,
+    )
     return pl.pallas_call(
         lambda *refs: deposit_kernel(blocks, cycles, nphi, nyquist, *refs),
-        out_shape=jax.ShapeDtypeStruct(whole, jnp.bfloat16),
-        in_specs=[pl.BlockSpec(memory_space=pltpu.SMEM)] + [pl.BlockSpec(memory_space=pltpu.HBM)] * 5,
-        out_specs=vmem,
+        out_shape=[
+            pltpu.VMEM(whole, jnp.bfloat16),
+            pltpu.VMEM(wigner.shape, wigner.dtype),
+            pltpu.VMEM(beam.shape, beam.dtype),
+        ],
+        in_specs=[pl.BlockSpec(memory_space=pltpu.SMEM)]
+        + [pl.BlockSpec(memory_space=pltpu.HBM)] * len(operands),
+        out_specs=[vmem] * 3,
         scratch_shapes=[
             pltpu.VMEM((rows, LANES), jnp.float32),
             pltpu.VMEM(coords.shape, jnp.float32),
             pltpu.VMEM((rows, LANES), jnp.int32),
             pltpu.VMEM((rows, LANES), jnp.int32),
-            pltpu.VMEM((6, rows, LANES), jnp.float32),
-            pltpu.VMEM((2 * cycles * blocks, chunk), jnp.bfloat16),
-            pltpu.VMEM((BLOCK, chunk), jnp.bfloat16),
-            pltpu.VMEM((2 * cycles * blocks, BLOCK), jnp.float32),
-            pltpu.VMEM(table.shape, jnp.bfloat16),
+            pltpu.VMEM((7, rows, LANES), jnp.float32),
+            pltpu.VMEM((2, channels * cycles * blocks, CHUNK), jnp.bfloat16),
+            pltpu.VMEM((2, BLOCK, CHUNK), jnp.bfloat16),
+            pltpu.VMEM((channels * cycles * blocks, BLOCK), jnp.float32),
+            pltpu.VMEM(table.shape, jnp.float32),
             pltpu.VMEM(whole, jnp.float32),
-            pltpu.SemaphoreType.DMA((5,)),
+            pltpu.SemaphoreType.DMA((len(operands),)),
         ],
-        compiler_params=pltpu.CompilerParams(vmem_limit_bytes=24 * 2**20),
-    )(
-        group,
-        values.reshape(rows, LANES),
-        coords,
-        cycle_ids.reshape(rows, LANES),
-        pixels.reshape(rows, LANES),
-        table,
-    )
+        compiler_params=pltpu.CompilerParams(vmem_limit_bytes=40 * 2**20),
+    )(group, *[pltpu.with_memory_space_constraint(x, pltpu.HBM) for x in operands])
 
 
 def project_kernel(scale, parts_ref, wigner_ref, beam_ref, out_ref, sky):
@@ -230,8 +270,7 @@
 
 
 def partial_sky(parts, wigner, beam, groups, scale):
-    orders, channels, cycles, waves = wigner.shape
-    pack = BLOCK // (channels * cycles)
+    orders, waves = parts.shape[1], beam.shape[1]
     vmem = pl.BlockSpec(memory_space=pltpu.VMEM)
     whole = (groups, 2 * orders * (waves // groups) // LANES, LANES)
     return pl.pallas_call(
@@ -240,8 +279,8 @@
         in_specs=[vmem] * 3,
         out_specs=vmem,
         scratch_shapes=[pltpu.VMEM((2 * orders, waves), jnp.float32)],
-        compiler_params=pltpu.CompilerParams(vmem_limit_bytes=24 * 2**20),
-    )(parts, wigner.reshape(orders // pack, BLOCK, waves), beam)
+        compiler_params=pltpu.CompilerParams(vmem_limit_bytes=16 * 2**20),
+    )(parts, wigner, beam)
 
 
 def finish_kernel(parts_ref, out_ref):
@@ -271,11 +310,12 @@
     nphi = 2 * tiles * orders
     nyquist = groups * channels // 2
     group = lax.axis_index("psi").astype(jnp.int32).reshape(1)
-    freq = partial_orders(
-        group, sample_values, sample_coords, tile_ids, phi_pixels, cycles, nphi, nyquist, tiles
+    samples = (sample_values, sample_coords, tile_ids, phi_pixels)
+    freq, wigner, beam = partial_orders(
+        group, *samples, wigner_table, beam, nphi, nyquist, tiles
     )
     freq = lax.all_to_all(freq, "theta", split_axis=0, concat_axis=0, tiled=True)
-    sky = partial_sky(freq, wigner_table, beam, groups, 1.0 / math.sqrt(groups * channels))
+    sky = partial_sky(freq, wigner, beam, groups, 1.0 / math.sqrt(groups * channels))
     sky = lax.all_to_all(sky, "psi", split_axis=0, concat_axis=0, tiled=True)
     return jnp.moveaxis(finish(sky, orders, waves // groups), 1, 0)
 

time: 55.6 us -> 46.2 us (0.83)
  local copies, waits for them, and re-layouts: 7.65 us -> 0 us
  Pallas kernels: 12.2 us -> 10.9 us
    unnamed x14 -> x0, local copies, waits for them, and re-layouts: 7.65 us -> none
    pallas_call x1, Pallas kernels: 9.14 us -> 7.78 us  [partial_orders(): pl.pallas_call(lambda *refs: deposit_kernel(blocks, cycles, nphi, nyquist...]
where the time goes in v2:
time: 46.2 us; the launch traced here: 45.8 us
  blocking collectives  34.9 us (76%)
  Pallas kernels  10.9 us (24%)
    all_to_all x1, blocking collectives, body(): sky = lax.all_to_all(sky, 'psi', split_axis=0, concat_axis=0, tiled=True)  19.1 us
    all_to_all x1, blocking collectives, body(): lax.all_to_all(freq, 'theta', split_axis=0, concat_axis=0, tiled=True)  15.8 us
    pallas_call x1, Pallas kernels, partial_orders(): pl.pallas_call(lambda *refs: deposit_kernel(blocks, cycles, nphi, nyquist...  7.78 us
    pallas_call x1, Pallas kernels, finish(): pl.pallas_call(finish_kernel, out_shape=jax.ShapeDtypeStruct((orders, 2,...  1.65 us
    pallas_call x1, Pallas kernels, partial_sky(): pl.pallas_call(lambda *refs: project_kernel(scale, *refs), out_shape=jax....  1.44 us

profile of v2, /device:TPU:2, one launch (start us, length us, event | category | flops | bytes accessed | tf_op | source)
XLA Modules:
  0.0 45.8 jit_solution(4688315289262263281)
XLA Ops:
  0.0 7.8 %shard_map.73 = (bf16[32,36,128]{2,1,0:T(8,128)(2,1)S(1)}, bf16[9,256,1152]{2,1,0:T(8,128)(2,1)S(1)}, f32[2,1152]{1,0:T(2,128)S(1)}) custom-call(s32[1]{0:T(128)} %bitcast.refs_0_, f32[64,128]{1,0:T(8,128)} %bitcast.7, f32[3,8192]{1,0:T(4,128)} %refs_2_.1, s32[64,128]{1,0:T(8,128)} %bitcast.8, s32[64,128]{1,0:T(8,128)} %bitcast.9, ...), custom_call_target="tpu_custom_call" | custom-call | tf_op jit(solution)/shard_map/pallas_call | solution.py:198
  7.8 15.8 %all_to_all.10.refs_0_ = bf16[32,36,128]{2,1,0:T(8,128)(2,1)S(1)} all-to-all(bf16[32,36,128]{2,1,0:T(8,128)(2,1)S(1)} %get-tuple-element.8), channel_id=1, replica_groups=mesh['psi'=8,'theta'=32] {'theta'}, dimensions={0} | all-to-all | bytes 589824 | tf_op jit(solution)/shard_map/all_to_all | solution.py:317
  23.6 1.4 %shard_map.74 = bf16[8,81,128]{2,1,0:T(8,128)(2,1)S(1)} custom-call(bf16[32,36,128]{2,1,0:T(8,128)(2,1)S(1)} %all_to_all.10.refs_0_, bf16[9,256,1152]{2,1,0:T(8,128)(2,1)S(1)} %get-tuple-element.9.refs_1_, f32[2,1152]{1,0:T(2,128)S(1)} %get-tuple-element.10.refs_2_), custom_call_target="tpu_custom_call" | custom-call | tf_op jit(solution)/shard_map/pallas_call | solution.py:276
  25.0 19.1 %all_to_all.11.parts_ref = bf16[8,81,128]{2,1,0:T(8,128)(2,1)} all-to-all(bf16[8,81,128]{2,1,0:T(8,128)(2,1)S(1)} %shard_map.74), channel_id=1, replica_groups=mesh['psi'=8,'theta'=32] {'psi'}, dimensions={0} | all-to-all | bytes 331776 | tf_op jit(solution)/shard_map/all_to_all | solution.py:319
  44.1 1.6 %shard_map.75 = f32[36,2,144]{2,1,0:T(2,128)} custom-call(bf16[8,81,128]{2,1,0:T(8,128)(2,1)} %all_to_all.11.parts_ref), custom_call_target="tpu_custom_call" | custom-call | tf_op jit(solution)/shard_map/pallas_call | solution.py:298

commit v3 on v2

--- a/solution.py
+++ b/solution.py
@@ -15,14 +15,24 @@
 CELLS = BLOCK // CELL
 STRIDE = OWNED * CELLS
 RADIX = 9
-CHUNK = 1024
+CHUNK = 4096
 NT = (((1,), (1,)), ((), ()))
 
 
+def members(k):
+    return [k] if k == 0 else [k, RADIX - k]
+
+
 def fourier_rows(nphi):
-    waves = np.arange(nphi // 2).reshape(-1, RADIX).T
-    phase = (2.0 * math.pi / nphi) * (waves[:, :, None] * (np.arange(BLOCK) - 1) % nphi)
-    return np.concatenate([np.cos(phase), np.sin(phase)], axis=2)
+    tables = []
+    for k in range(RADIX // 2 + 1):
+        for m in members(k):
+            waves = np.arange(m, nphi // 2, RADIX)
+            phase = (2.0 * math.pi / nphi) * (waves[:, None] * (np.arange(BLOCK) - 1) % nphi)
+            tables.append(
+                np.concatenate([np.cos(phase), (1.0 if m == k else -1.0) * np.sin(phase)], axis=1)
+            )
+    return np.concatenate(tables, axis=0)
 
 
 def phase_sums(runs):
@@ -40,6 +50,16 @@
                 imag = part if imag is None else imag + part
         sums.append((real, imag))
     return sums
+
+
+def sine_of_turns(x):
+    x = jnp.where(jnp.abs(x) > 0.25, jnp.where(x > 0, 0.5, -0.5) - x, x)
+    y = (2.0 * math.pi) * x
+    square = y * y
+    total = jnp.full_like(y, -1.0 / math.factorial(11))
+    for k in (9, 7, 5, 3, 1):
+        total = total * square + (-1.0) ** (k // 2) / math.factorial(k)
+    return total * y
 
 
 def split(x):
@@ -71,12 +91,13 @@
     cycle_frac, pixel_frac, turns = fields[0], fields[1], fields[2]
     value = values[...]
 
-    def angle(harmonic):
+    def sine(harmonic, shift):
         phase = turns * harmonic.astype(jnp.float32)
-        return (2.0 * math.pi) * (phase - jnp.round(phase))
-
-    even = jnp.where(group == 0, 1.0, 2.0 * jnp.sin(angle(group))) * value
-    odd = jnp.where(group == nyquist - 1, 1.0, 2.0) * jnp.cos(angle(group + 1)) * value
+        phase = phase - jnp.round(phase) + shift
+        return sine_of_turns(phase - jnp.round(phase))
+
+    even = jnp.where(group == 0, 1.0, 2.0 * sine(group, 0.0)) * value
+    odd = jnp.where(group == nyquist - 1, 1.0, 2.0) * sine(group + 1, 0.25) * value
     pixel = pixels[...]
     cell = (pixel.astype(jnp.float32) * (1.0 / OWNED) + 0.5 / OWNED).astype(jnp.int32)
     fields[0] = even * (1.0 - cycle_frac)
@@ -89,9 +110,9 @@
     copies[3].wait()
     cycle_ids = lax.broadcasted_iota(jnp.int32, (cycles, LANES), 0)
     columns = 0.5 * lax.broadcasted_iota(jnp.int32, (CELL, LANES), 0).astype(jnp.float32)
-    width = left.shape[2] // LANES
-
-    def fill(step, slot):
+    width = left.shape[1] // LANES
+
+    def chunk(step, carry):
         for j in range(width):
             row = pl.ds(step * width + j, 1)
             lanes = slice(j * LANES, (j + 1) * LANES)
@@ -110,36 +131,27 @@
                 mine = own == jnp.bfloat16(b)
                 for c in range(2):
                     start = (2 * b + c) * cycles
-                    left[slot, start : start + cycles, lanes] = jnp.where(mine, hats[c], jnp.bfloat16(0))
+                    left[start : start + cycles, lanes] = jnp.where(mine, hats[c], jnp.bfloat16(0))
             offset = columns - fields[1, row, :]
             inner = jnp.maximum(1.0 - offset * offset, 0.0)
             taps = (inner * inner).astype(jnp.bfloat16)
             for q in range(CELLS):
-                right[slot, q * CELL : (q + 1) * CELL, lanes] = jnp.where(
+                right[q * CELL : (q + 1) * CELL, lanes] = jnp.where(
                     within == jnp.bfloat16(q), taps, jnp.bfloat16(0)
                 )
-
-    def add(slot):
         cube[...] += lax.dot_general(
-            left[slot], right[slot], NT, preferred_element_type=jnp.float32
-        )
-
-    steps = rows // width
-    fill(0, 0)
-
-    def pair(step, carry):
-        fill(2 * step + 1, 1)
-        add(0)
-        fill(jnp.minimum(2 * step + 2, steps - 1), 0)
-        add(1)
+            left[...], right[...], NT, preferred_element_type=jnp.float32
+        )
         return carry
 
-    lax.fori_loop(0, steps // 2, pair, 0)
+    lax.fori_loop(0, rows // width, chunk, 0)
     source = lax.broadcasted_iota(jnp.int32, (BLOCK, BLOCK), 0)
     target = lax.broadcasted_iota(jnp.int32, (BLOCK, BLOCK), 1)
     join = (source - 3 * (source // CELL) == target).astype(jnp.bfloat16)
-    cube[...] = sum(
-        jnp.dot(part, join, preferred_element_type=jnp.float32) for part in split(cube[...])
+    cube[...] = jnp.dot(
+        jnp.concatenate(split(cube[...]), axis=1),
+        jnp.concatenate([join, join], axis=0),
+        preferred_element_type=jnp.float32,
     )
     lines = 2 * cycles
     tiles = nphi // LANES
@@ -160,19 +172,34 @@
     groups = phase_sums(runs)
     copies[4].wait()
     share = out_ref.shape[1] // RADIX
-    for m in range(RADIX):
-        real, imag = groups[min(m, RADIX - m)]
-        imag = jnp.zeros_like(real) if m == 0 else (imag if m <= RADIX // 2 else -imag)
+    count = table.shape[0] // RADIX
+    conjugate = jnp.where(
+        lax.broadcasted_iota(jnp.int32, (1, LANES), 1) < lines, 1.0, -1.0
+    )
+    start = 0
+    for k, (real, imag) in enumerate(groups):
+        real = split(real * (1.0 / math.sqrt(nphi)))
+        imag = split(jnp.zeros_like(real[0], jnp.float32) if k == 0 else imag * (1.0 / math.sqrt(nphi)))
         operand = jnp.concatenate(
-            [jnp.concatenate([real, imag], axis=1), jnp.concatenate([imag, -real], axis=1)], axis=0
-        ) * (1.0 / math.sqrt(nphi))
-        waves_m = table[m].astype(jnp.bfloat16)
-        waves = sum(
-            lax.dot_general(waves_m, part, NT, preferred_element_type=jnp.float32)
-            for part in split(operand)
-        )
-        for d in range(out_ref.shape[0]):
-            spread[d, m * share : (m + 1) * share, :] = waves[d * share : (d + 1) * share]
+            [
+                jnp.concatenate(pair, axis=1)
+                for r, i in zip(real, imag)
+                for pair in ((r, i), (i, -r))
+            ],
+            axis=0,
+        )
+        stop = start + count * len(members(k))
+        both = lax.dot_general(
+            table[start:stop].astype(jnp.bfloat16), operand, NT, preferred_element_type=jnp.float32
+        )
+        start = stop
+        both = both[:, :LANES] + both[:, LANES:]
+        for place, m in enumerate(members(k)):
+            waves = both[place * count : (place + 1) * count]
+            if place:
+                waves = waves * conjugate
+            for d in range(out_ref.shape[0]):
+                spread[d, m * share : (m + 1) * share, :] = waves[d * share : (d + 1) * share]
     out_ref[...] = spread[...].astype(jnp.bfloat16)
     for copy in copies[5:]:
         copy.wait()
@@ -211,8 +238,8 @@
             pltpu.VMEM((rows, LANES), jnp.int32),
             pltpu.VMEM((rows, LANES), jnp.int32),
             pltpu.VMEM((7, rows, LANES), jnp.float32),
-            pltpu.VMEM((2, channels * cycles * blocks, CHUNK), jnp.bfloat16),
-            pltpu.VMEM((2, BLOCK, CHUNK), jnp.bfloat16),
+            pltpu.VMEM((channels * cycles * blocks, CHUNK), jnp.bfloat16),
+            pltpu.VMEM((BLOCK, CHUNK), jnp.bfloat16),
             pltpu.VMEM((channels * cycles * blocks, BLOCK), jnp.float32),
             pltpu.VMEM(table.shape, jnp.float32),
             pltpu.VMEM(whole, jnp.float32),
@@ -300,6 +327,7 @@
         out_shape=jax.ShapeDtypeStruct((orders, 2, waves), jnp.float32),
         in_specs=[vmem],
         out_specs=vmem,
+        compiler_params=pltpu.CompilerParams(vmem_limit_bytes=2 * 2**20),
     )(parts)
 
 

time: 46.2 us -> 44.1 us (0.955)
  Pallas kernels: 10.9 us -> 8.82 us
    pallas_call x1, Pallas kernels: 7.78 us -> 6.64 us  [partial_orders(): pl.pallas_call(lambda *refs: deposit_kernel(blocks, cycles, nphi, nyquist...]
    pallas_call x1, Pallas kernels: 1.65 us -> 0.73 us  [finish(): pl.pallas_call(finish_kernel, out_shape=jax.ShapeDtypeStruct((orders, 2,...]
where the time goes in v3:
time: 44.1 us; the launch traced here: 43.6 us
  blocking collectives  34.8 us (79%)
  Pallas kernels  8.82 us (20%)
    all_to_all x1, blocking collectives, body(): sky = lax.all_to_all(sky, 'psi', split_axis=0, concat_axis=0, tiled=True)  19 us
    all_to_all x1, blocking collectives, body(): lax.all_to_all(freq, 'theta', split_axis=0, concat_axis=0, tiled=True)  15.8 us
    pallas_call x1, Pallas kernels, partial_orders(): pl.pallas_call(lambda *refs: deposit_kernel(blocks, cycles, nphi, nyquist...  6.64 us
    pallas_call x1, Pallas kernels, partial_sky(): pl.pallas_call(lambda *refs: project_kernel(scale, *refs), out_shape=jax....  1.44 us

profile of v3, /device:TPU:2, one launch (start us, length us, event | category | flops | bytes accessed | tf_op | source)
XLA Modules:
  0.0 43.6 jit_solution(14901203585508812743)
XLA Ops:
  0.0 6.6 %shard_map.73 = (bf16[32,36,128]{2,1,0:T(8,128)(2,1)S(1)}, bf16[9,256,1152]{2,1,0:T(8,128)(2,1)S(1)}, f32[2,1152]{1,0:T(2,128)S(1)}) custom-call(s32[1]{0:T(128)} %bitcast.refs_0_, f32[64,128]{1,0:T(8,128)} %bitcast.7, f32[3,8192]{1,0:T(4,128)} %refs_2_.1, s32[64,128]{1,0:T(8,128)} %bitcast.8, s32[64,128]{1,0:T(8,128)} %bitcast.9, ...), custom_call_target="tpu_custom_call" | custom-call | tf_op jit(solution)/shard_map/pallas_call | solution.py:225
  6.7 15.8 %all_to_all.10.refs_0_ = bf16[32,36,128]{2,1,0:T(8,128)(2,1)S(1)} all-to-all(bf16[32,36,128]{2,1,0:T(8,128)(2,1)S(1)} %get-tuple-element.8), channel_id=1, replica_groups=mesh['psi'=8,'theta'=32] {'theta'}, dimensions={0} | all-to-all | bytes 589824 | tf_op jit(solution)/shard_map/all_to_all | solution.py:345
  22.5 1.4 %shard_map.74 = bf16[8,81,128]{2,1,0:T(8,128)(2,1)S(1)} custom-call(bf16[32,36,128]{2,1,0:T(8,128)(2,1)S(1)} %all_to_all.10.refs_0_, bf16[9,256,1152]{2,1,0:T(8,128)(2,1)S(1)} %get-tuple-element.9.refs_1_, f32[2,1152]{1,0:T(2,128)S(1)} %get-tuple-element.10.refs_2_), custom_call_target="tpu_custom_call" | custom-call | tf_op jit(solution)/shard_map/pallas_call | solution.py:303
  23.9 19.0 %all_to_all.11.parts_ref = bf16[8,81,128]{2,1,0:T(8,128)(2,1)S(1)} all-to-all(bf16[8,81,128]{2,1,0:T(8,128)(2,1)S(1)} %shard_map.74), channel_id=1, replica_groups=mesh['psi'=8,'theta'=32] {'psi'}, dimensions={0} | all-to-all | bytes 331776 | tf_op jit(solution)/shard_map/all_to_all | solution.py:347
  42.9 0.7 %shard_map.75 = f32[36,2,144]{2,1,0:T(2,128)} custom-call(bf16[8,81,128]{2,1,0:T(8,128)(2,1)S(1)} %all_to_all.11.parts_ref), custom_call_target="tpu_custom_call" | custom-call | tf_op jit(solution)/shard_map/pallas_call | solution.py:325

commit v4 on v3

--- a/solution.py
+++ b/solution.py
@@ -68,8 +68,8 @@
 
 
 def deposit_kernel(
-    blocks, cycles, nphi, nyquist, psi_ref, v_hbm, coords_hbm, t_hbm, o_hbm, table_hbm, wigner_hbm,
-    beam_hbm, out_ref, wigner, beam, values, coords, cycle_of, pixels, fields, left, right, cube,
+    blocks, cycles, nphi, nyquist, place_ref, v_hbm, coords_hbm, t_hbm, o_hbm, table_hbm, wigner_hbm,
+    beam_hbm, own_ref, other_ref, wigner, beam, values, coords, cycle_of, pixels, fields, left, right, cube,
     table, spread, sems,
 ):
     sources = (v_hbm, coords_hbm, o_hbm, t_hbm, table_hbm, beam_hbm, wigner_hbm)
@@ -81,7 +81,7 @@
     for copy in copies:
         copy.start()
     cube[...] = jnp.zeros_like(cube)
-    group = psi_ref[0]
+    group, core = place_ref[0] >> 1, place_ref[0] & 1
     for copy in copies[:3]:
         copy.wait()
     rows = values.shape[0]
@@ -171,7 +171,7 @@
     runs = [jnp.concatenate(sums[b * per_run : (b + 1) * per_run], axis=1) for b in range(RADIX)]
     groups = phase_sums(runs)
     copies[4].wait()
-    share = out_ref.shape[1] // RADIX
+    half, share = own_ref.shape[0], own_ref.shape[1] // RADIX
     count = table.shape[0] // RADIX
     conjugate = jnp.where(
         lax.broadcasted_iota(jnp.int32, (1, LANES), 1) < lines, 1.0, -1.0
@@ -198,14 +198,16 @@
             waves = both[place * count : (place + 1) * count]
             if place:
                 waves = waves * conjugate
-            for d in range(out_ref.shape[0]):
-                spread[d, m * share : (m + 1) * share, :] = waves[d * share : (d + 1) * share]
-    out_ref[...] = spread[...].astype(jnp.bfloat16)
+            for d in range(2 * half):
+                slot = d % 2 * half + d // 2
+                spread[slot, m * share : (m + 1) * share, :] = waves[d * share : (d + 1) * share]
+    own_ref[...] = spread[pl.ds(core * half, half)].astype(jnp.bfloat16)
+    other_ref[...] = spread[pl.ds((1 - core) * half, half)].astype(jnp.bfloat16)
     for copy in copies[5:]:
         copy.wait()
 
 
-def partial_orders(group, values, coords, cycle_ids, pixels, wigner, beam, nphi, nyquist, tiles):
+def partial_orders(place, values, coords, cycle_ids, pixels, wigner, beam, nphi, nyquist, tiles):
     orders, channels, cycles, waves = wigner.shape
     blocks = -(-nphi // STRIDE)
     rows = values.shape[0] // LANES
@@ -225,13 +227,14 @@
     return pl.pallas_call(
         lambda *refs: deposit_kernel(blocks, cycles, nphi, nyquist, *refs),
         out_shape=[
-            pltpu.VMEM(whole, jnp.bfloat16),
+            pltpu.VMEM((tiles // 2, *whole[1:]), jnp.bfloat16),
+            pltpu.VMEM((tiles // 2, *whole[1:]), jnp.bfloat16),
             pltpu.VMEM(wigner.shape, wigner.dtype),
             pltpu.VMEM(beam.shape, beam.dtype),
         ],
         in_specs=[pl.BlockSpec(memory_space=pltpu.SMEM)]
         + [pl.BlockSpec(memory_space=pltpu.HBM)] * len(operands),
-        out_specs=[vmem] * 3,
+        out_specs=[vmem] * 4,
         scratch_shapes=[
             pltpu.VMEM((rows, LANES), jnp.float32),
             pltpu.VMEM(coords.shape, jnp.float32),
@@ -246,7 +249,7 @@
             pltpu.SemaphoreType.DMA((len(operands),)),
         ],
         compiler_params=pltpu.CompilerParams(vmem_limit_bytes=40 * 2**20),
-    )(group, *[pltpu.with_memory_space_constraint(x, pltpu.HBM) for x in operands])
+    )(place, *[pltpu.with_memory_space_constraint(x, pltpu.HBM) for x in operands])
 
 
 def project_kernel(scale, parts_ref, wigner_ref, beam_ref, out_ref, sky):
@@ -337,12 +340,17 @@
     orders, channels, cycles, waves = wigner_table.shape
     nphi = 2 * tiles * orders
     nyquist = groups * channels // 2
-    group = lax.axis_index("psi").astype(jnp.int32).reshape(1)
+    place = (2 * lax.axis_index("psi") + (lax.axis_index("theta") & 1)).astype(jnp.int32).reshape(1)
     samples = (sample_values, sample_coords, tile_ids, phi_pixels)
-    freq, wigner, beam = partial_orders(
-        group, *samples, wigner_table, beam, nphi, nyquist, tiles
-    )
-    freq = lax.all_to_all(freq, "theta", split_axis=0, concat_axis=0, tiled=True)
+    own, other, wigner, beam = partial_orders(
+        place, *samples, wigner_table, beam, nphi, nyquist, tiles
+    )
+    arrived = lax.ppermute(other, "theta", [(i, i ^ 1) for i in range(tiles)])
+    freq = (own.astype(jnp.float32) + arrived.astype(jnp.float32)).astype(jnp.bfloat16)
+    sides = [list(range(side, tiles, 2)) for side in range(2)]
+    freq = lax.all_to_all(
+        freq, "theta", split_axis=0, concat_axis=0, axis_index_groups=sides, tiled=True
+    )
     sky = partial_sky(freq, wigner, beam, groups, 1.0 / math.sqrt(groups * channels))
     sky = lax.all_to_all(sky, "psi", split_axis=0, concat_axis=0, tiled=True)
     return jnp.moveaxis(finish(sky, orders, waves // groups), 1, 0)

time: 44.1 us -> 42.5 us (0.964)
  blocking collectives: 34.8 us -> 31.9 us
  waiting for transfers between devices: 0 us -> 1.38 us
    all_to_all x1, blocking collectives: 15.8 us -> 14.1 us  [body(): lax.all_to_all(freq, 'theta', split_axis=0, concat_axis=0, axis_index_gro...]
    ppermute x0 -> x1, waiting for transfers between devices: none -> 1.38 us  [body(): arrived = lax.ppermute(other, 'theta', [(i, i ^ 1) for i in range(tiles)])]
    all_to_all x1, blocking collectives: 19 us -> 17.9 us  [body(): sky = lax.all_to_all(sky, 'psi', split_axis=0, concat_axis=0, tiled=True)]
  transfers between devices with their start and end apart: 0 -> 1, of which waited for: 0 -> 1; matrix products, arithmetic and copies ran while one was open for 0% -> 0% of each run, Pallas kernels for 0% -> 0%
where the time goes in v4:
time: 42.5 us; the launch traced here: 42.3 us
  blocking collectives  31.9 us (75%)
  Pallas kernels  8.81 us (21%)
  waiting for transfers between devices  1.38 us (3%)
    all_to_all x1, blocking collectives, body(): sky = lax.all_to_all(sky, 'psi', split_axis=0, concat_axis=0, tiled=True)  17.9 us
    all_to_all x1, blocking collectives, body(): lax.all_to_all(freq, 'theta', split_axis=0, concat_axis=0, axis_index_gro...  14.1 us
    pallas_call x1, Pallas kernels, partial_orders(): pl.pallas_call(lambda *refs: deposit_kernel(blocks, cycles, nphi, nyquist...  6.67 us
    pallas_call x1, Pallas kernels, partial_sky(): pl.pallas_call(lambda *refs: project_kernel(scale, *refs), out_shape=jax....  1.41 us
    ppermute x1, waiting for transfers between devices, body(): arrived = lax.ppermute(other, 'theta', [(i, i ^ 1) for i in range(tiles)])  1.38 us
  transfers between devices with their start and end apart: 1, of which 1 were waited for; matrix products, arithmetic and copies ran while one was open for 0% of the time, Pallas kernels for 0%

profile of v4, /device:TPU:2, one launch (start us, length us, event | category | flops | bytes accessed | tf_op | source)
XLA Modules:
  0.0 42.3 jit_solution(11538174255524308628)
XLA Ops:
  0.0 6.7 %shard_map.73 = (bf16[16,36,128]{2,1,0:T(8,128)(2,1)S(1)}, bf16[16,36,128]{2,1,0:T(8,128)(2,1)S(1)}, bf16[9,256,1152]{2,1,0:T(8,128)(2,1)S(1)}, f32[2,1152]{1,0:T(2,128)S(1)}) custom-call(s32[1]{0:T(128)} %bitcast.refs_0_, f32[64,128]{1,0:T(8,128)} %bitcast.7, f32[3,8192]{1,0:T(4,128)} %refs_2_.1, s32[64,128]{1,0:T(8,128)} %bitcast.8, s32[64,128]{1,0:T(8,128)} %bitcast.9, ...), custom_call_target="tpu_custom_call" | custom-call | tf_op jit(solution)/shard_map/pallas_call | solution.py:227
  6.7 0.1 collective-permute-start
  6.8 1.4 %collective-permute-done = bf16[16,36,128]{2,1,0:T(8,128)(2,1)S(1)} collective-permute-done((bf16[16,36,128]{2,1,0:T(8,128)(2,1)S(1)}, bf16[16,36,128]{2,1,0:T(8,128)(2,1)S(1)}, u32[]{:S(2)}, u32[]{:S(2)}) %collective-permute-start) | collective-permute-done | bytes 147488 | tf_op jit(solution)/shard_map/ppermute | solution.py:348
  8.2 14.1 %all_to_all.10.refs_0_ = bf16[16,36,128]{2,1,0:T(8,128)(2,1)S(1)} all-to-all(bf16[16,36,128]{2,1,0:T(8,128)(2,1)S(1)} %add_convert_fusion), channel_id=1, replica_groups={{0,2,4,6,8,10,12,14,16,18,20,22,24,26,28,30},{1,3,5,7,9,11,13,15,17,19,..., dimensions={0} | all-to-all | bytes 294912 | tf_op jit(solution)/shard_map/all_to_all | solution.py:351
  22.3 1.4 %shard_map.74 = bf16[8,81,128]{2,1,0:T(8,128)(2,1)S(1)} custom-call(bf16[16,36,128]{2,1,0:T(8,128)(2,1)S(1)} %all_to_all.10.refs_0_, bf16[9,256,1152]{2,1,0:T(8,128)(2,1)S(1)} %get-tuple-element.11.refs_1_, f32[2,1152]{1,0:T(2,128)S(1)} %get-tuple-element.12.refs_2_), custom_call_target="tpu_custom_call" | custom-call | tf_op jit(solution)/shard_map/pallas_call | solution.py:306
  23.7 17.9 %all_to_all.11.parts_ref = bf16[8,81,128]{2,1,0:T(8,128)(2,1)S(1)} all-to-all(bf16[8,81,128]{2,1,0:T(8,128)(2,1)S(1)} %shard_map.74), channel_id=1, replica_groups=mesh['psi'=8,'theta'=32] {'psi'}, dimensions={0} | all-to-all | bytes 331776 | tf_op jit(solution)/shard_map/all_to_all | solution.py:355
  41.6 0.7 %shard_map.75 = f32[36,2,144]{2,1,0:T(2,128)} custom-call(bf16[8,81,128]{2,1,0:T(8,128)(2,1)S(1)} %all_to_all.11.parts_ref), custom_call_target="tpu_custom_call" | custom-call | tf_op jit(solution)/shard_map/pallas_call | solution.py:328
  (1 shorter events, 0.0 us)
Async XLA Ops:
  6.7 1.5 %collective-permute-start = (bf16[16,36,128]{2,1,0:T(8,128)(2,1)S(1)}, bf16[16,36,128]{2,1,0:T(8,128)(2,1)S(1)}, u32[]{:S(2)}, u32[]{:S(2)}) collective-permute-start(bf16[16,36,128]{2,1,0:T(8,128)(2,1)S(1)} %get-tuple-element.10), channel_id=1, source_target_pairs={{0,1},{1,0},{2,3},{3,2},{4,5},{5,4},{6,7},{7,6},{8,9},{9,8},{10,11... | collective-permute-start | bytes 442376 | tf_op jit(solution)/shard_map/ppermute | solution.py:348

commit v5 on v4

--- a/solution.py
+++ b/solution.py
@@ -60,6 +60,11 @@
     for k in (9, 7, 5, 3, 1):
         total = total * square + (-1.0) ** (k // 2) / math.factorial(k)
     return total * y
+
+
+def log2(size):
+    assert size == 1 << size.bit_length() - 1
+    return size.bit_length() - 1
 
 
 def split(x):
@@ -105,8 +110,8 @@
     fields[4] = odd * (1.0 - cycle_frac)
     fields[5] = odd * cycle_frac
     fields[1] = 0.5 * ((pixel - OWNED * cell + 1).astype(jnp.float32) + pixel_frac)
-    fields[2] = (cell // CELLS).astype(jnp.float32)
-    fields[6] = (cell % CELLS).astype(jnp.float32)
+    fields[2] = (cell >> log2(CELLS)).astype(jnp.float32)
+    fields[6] = (cell & CELLS - 1).astype(jnp.float32)
     copies[3].wait()
     cycle_ids = lax.broadcasted_iota(jnp.int32, (cycles, LANES), 0)
     columns = 0.5 * lax.broadcasted_iota(jnp.int32, (CELL, LANES), 0).astype(jnp.float32)
@@ -147,7 +152,7 @@
     lax.fori_loop(0, rows // width, chunk, 0)
     source = lax.broadcasted_iota(jnp.int32, (BLOCK, BLOCK), 0)
     target = lax.broadcasted_iota(jnp.int32, (BLOCK, BLOCK), 1)
-    join = (source - 3 * (source // CELL) == target).astype(jnp.bfloat16)
+    join = (source - 3 * (source >> log2(CELL)) == target).astype(jnp.bfloat16)
     cube[...] = jnp.dot(
         jnp.concatenate(split(cube[...]), axis=1),
         jnp.concatenate([join, join], axis=0),
@@ -252,28 +257,25 @@
     )(place, *[pltpu.with_memory_space_constraint(x, pltpu.HBM) for x in operands])
 
 
-def project_kernel(scale, parts_ref, wigner_ref, beam_ref, out_ref, sky):
+def project_kernel(scale, parts_ref, wigner_ref, beam_ref, out_ref, sky, tall):
     orders, lanes = parts_ref.shape[1:]
     depth = lanes // 2
     pack = BLOCK // depth
-    summed = split(jnp.sum(parts_ref[...].astype(jnp.float32), axis=0))
-    row = lax.broadcasted_iota(jnp.int32, (2 * orders, orders), 0)
-    place = lax.broadcasted_iota(jnp.int32, (2 * orders, orders), 1)
-    order = row // 2
-    found = (order % RADIX) * (orders // RADIX) + order // RADIX == place
-    chosen = [(found & (row % 2 == x)).astype(jnp.bfloat16) for x in range(2)]
+    summed = jnp.sum(parts_ref[...].astype(jnp.float32), axis=0)
+    share = orders // RADIX
+    for m in range(RADIX):
+        for x in range(2):
+            tall[pl.ds(2 * m + x, share, stride=2 * RADIX), :] = summed[
+                m * share : (m + 1) * share, x * depth : (x + 1) * depth
+            ]
     row = lax.broadcasted_iota(jnp.int32, (2 * orders, BLOCK), 0)
     lane = lax.broadcasted_iota(jnp.int32, (2 * orders, BLOCK), 1)
-    mine = row // 2 % pack == lane // depth
-    second = lane // (depth // 2) % 2
-    tops = []
-    for part in summed:
-        tall = sum(
-            jnp.dot(chosen[x], part[:, x * depth : (x + 1) * depth], preferred_element_type=jnp.float32)
-            for x in range(2)
-        )
-        wide = jnp.concatenate([tall] * pack, axis=1)
-        tops += [jnp.where(mine & (second == c), wide, 0.0) for c in range(2)]
+    mine = (row >> 1 & pack - 1) == lane >> log2(depth)
+    second = lane >> log2(depth // 2) & 1
+    wide = jnp.where(mine, jnp.concatenate([tall[...]] * pack, axis=1), 0.0)
+    tops = [
+        jnp.where(second == c, part.astype(jnp.float32), 0.0) for part in split(wide) for c in range(2)
+    ]
     beam = beam_ref[...] * scale
     height = 2 * pack
     for g in range(orders // pack):
@@ -308,7 +310,10 @@
         out_shape=jax.ShapeDtypeStruct(whole, jnp.bfloat16),
         in_specs=[vmem] * 3,
         out_specs=vmem,
-        scratch_shapes=[pltpu.VMEM((2 * orders, waves), jnp.float32)],
+        scratch_shapes=[
+            pltpu.VMEM((2 * orders, waves), jnp.float32),
+            pltpu.VMEM((2 * orders, parts.shape[2] // 2), jnp.float32),
+        ],
         compiler_params=pltpu.CompilerParams(vmem_limit_bytes=16 * 2**20),
     )(parts, wigner, beam)
 

time: 42.5 us -> 42.3 us (level)
  no operation moved by 1% of the time
where the time goes in v5:
time: 42.3 us; the launch traced here: 42.1 us
  blocking collectives  31.9 us (75%)
  Pallas kernels  8.65 us (20%)
  waiting for transfers between devices  1.38 us (3%)
    all_to_all x1, blocking collectives, body(): sky = lax.all_to_all(sky, 'psi', split_axis=0, concat_axis=0, tiled=True)  17.9 us
    all_to_all x1, blocking collectives, body(): lax.all_to_all(freq, 'theta', split_axis=0, concat_axis=0, axis_index_gro...  14.1 us
    pallas_call x1, Pallas kernels, partial_orders(): pl.pallas_call(lambda *refs: deposit_kernel(blocks, cycles, nphi, nyquist...  6.65 us
    ppermute x1, waiting for transfers between devices, body(): arrived = lax.ppermute(other, 'theta', [(i, i ^ 1) for i in range(tiles)])  1.38 us
    pallas_call x1, Pallas kernels, partial_sky(): pl.pallas_call(lambda *refs: project_kernel(scale, *refs), out_shape=jax....  1.27 us
  transfers between devices with their start and end apart: 1, of which 1 were waited for; matrix products, arithmetic and copies ran while one was open for 0% of the time, Pallas kernels for 0%

profile of v5, /device:TPU:2, one launch (start us, length us, event | category | flops | bytes accessed | tf_op | source)
XLA Modules:
  0.0 42.1 jit_solution(11016794690354232216)
XLA Ops:
  0.0 6.7 %shard_map.73 = (bf16[16,36,128]{2,1,0:T(8,128)(2,1)S(1)}, bf16[16,36,128]{2,1,0:T(8,128)(2,1)S(1)}, bf16[9,256,1152]{2,1,0:T(8,128)(2,1)S(1)}, f32[2,1152]{1,0:T(2,128)S(1)}) custom-call(s32[1]{0:T(128)} %bitcast.refs_0_, f32[64,128]{1,0:T(8,128)} %bitcast.7, f32[3,8192]{1,0:T(4,128)} %refs_2_.1, s32[64,128]{1,0:T(8,128)} %bitcast.8, s32[64,128]{1,0:T(8,128)} %bitcast.9, ...), custom_call_target="tpu_custom_call" | custom-call | tf_op jit(solution)/shard_map/pallas_call | solution.py:232
  6.7 0.1 collective-permute-start
  6.8 1.4 %collective-permute-done = bf16[16,36,128]{2,1,0:T(8,128)(2,1)S(1)} collective-permute-done((bf16[16,36,128]{2,1,0:T(8,128)(2,1)S(1)}, bf16[16,36,128]{2,1,0:T(8,128)(2,1)S(1)}, u32[]{:S(2)}, u32[]{:S(2)}) %collective-permute-start) | collective-permute-done | bytes 147488 | tf_op jit(solution)/shard_map/ppermute | solution.py:353
  8.2 14.1 %all_to_all.10.refs_0_ = bf16[16,36,128]{2,1,0:T(8,128)(2,1)S(1)} all-to-all(bf16[16,36,128]{2,1,0:T(8,128)(2,1)S(1)} %add_convert_fusion), channel_id=1, replica_groups={{0,2,4,6,8,10,12,14,16,18,20,22,24,26,28,30},{1,3,5,7,9,11,13,15,17,19,..., dimensions={0} | all-to-all | bytes 294912 | tf_op jit(solution)/shard_map/all_to_all | solution.py:356
  22.3 1.3 %shard_map.74 = bf16[8,81,128]{2,1,0:T(8,128)(2,1)S(1)} custom-call(bf16[16,36,128]{2,1,0:T(8,128)(2,1)S(1)} %all_to_all.10.refs_0_, bf16[9,256,1152]{2,1,0:T(8,128)(2,1)S(1)} %get-tuple-element.11.refs_1_, f32[2,1152]{1,0:T(2,128)S(1)} %get-tuple-element.12.refs_2_), custom_call_target="tpu_custom_call" | custom-call | tf_op jit(solution)/shard_map/pallas_call | solution.py:308
  23.5 17.9 %all_to_all.11.parts_ref = bf16[8,81,128]{2,1,0:T(8,128)(2,1)S(1)} all-to-all(bf16[8,81,128]{2,1,0:T(8,128)(2,1)S(1)} %shard_map.74), channel_id=1, replica_groups=mesh['psi'=8,'theta'=32] {'psi'}, dimensions={0} | all-to-all | bytes 331776 | tf_op jit(solution)/shard_map/all_to_all | solution.py:360
  41.4 0.7 %shard_map.75 = f32[36,2,144]{2,1,0:T(2,128)} custom-call(bf16[8,81,128]{2,1,0:T(8,128)(2,1)S(1)} %all_to_all.11.parts_ref), custom_call_target="tpu_custom_call" | custom-call | tf_op jit(solution)/shard_map/pallas_call | solution.py:333
  (1 shorter events, 0.0 us)
Async XLA Ops:
  6.7 1.5 %collective-permute-start = (bf16[16,36,128]{2,1,0:T(8,128)(2,1)S(1)}, bf16[16,36,128]{2,1,0:T(8,128)(2,1)S(1)}, u32[]{:S(2)}, u32[]{:S(2)}) collective-permute-start(bf16[16,36,128]{2,1,0:T(8,128)(2,1)S(1)} %get-tuple-element.10), channel_id=1, source_target_pairs={{0,1},{1,0},{2,3},{3,2},{4,5},{5,4},{6,7},{7,6},{8,9},{9,8},{10,11... | collective-permute-start | bytes 442376 | tf_op jit(solution)/shard_map/ppermute | solution.py:353

commit v6 on v5

--- a/solution.py
+++ b/solution.py
@@ -23,7 +23,7 @@
     return [k] if k == 0 else [k, RADIX - k]
 
 
-def fourier_rows(nphi):
+def fourier_rows(nphi, tiles):
     tables = []
     for k in range(RADIX // 2 + 1):
         for m in members(k):
@@ -32,7 +32,8 @@
             tables.append(
                 np.concatenate([np.cos(phase), (1.0 if m == k else -1.0) * np.sin(phase)], axis=1)
             )
-    return np.concatenate(tables, axis=0)
+    sides = [x.reshape(tiles // 2, 2, -1, 2 * BLOCK).swapaxes(0, 1).reshape(2, -1, 2 * BLOCK) for x in tables]
+    return np.concatenate(sides, axis=1)
 
 
 def phase_sums(runs):
@@ -72,10 +73,52 @@
     return high, (x - high.astype(jnp.float32)).astype(jnp.bfloat16)
 
 
+def transform(table, operands, out_ref, spread):
+    owners, share = out_ref.shape[0], out_ref.shape[1] // RADIX
+    count = owners * share
+    conjugate = jnp.where(
+        lax.broadcasted_iota(jnp.int32, (1, LANES), 1) < LANES // 2, 1.0, -1.0
+    )
+    start = 0
+    for k in range(operands.shape[0]):
+        stop = start + count * len(members(k))
+        both = lax.dot_general(
+            table[start:stop].astype(jnp.bfloat16),
+            operands[k],
+            NT,
+            preferred_element_type=jnp.float32,
+        )
+        start = stop
+        both = both[:, :LANES] + both[:, LANES:]
+        for place, m in enumerate(members(k)):
+            waves = both[place * count : (place + 1) * count]
+            if place:
+                waves = waves * conjugate
+            for d in range(owners):
+                spread[d, m * share : (m + 1) * share, :] = waves[d * share : (d + 1) * share]
+    out_ref[...] = spread[...].astype(jnp.bfloat16)
+
+
+def own_kernel(place_ref, table, operands, own_ref, spread):
+    transform(table.at[place_ref[0] & 1], operands, own_ref, spread)
+
+
+def own_orders(place, table, operands, shape):
+    vmem = pl.BlockSpec(memory_space=pltpu.VMEM)
+    return pl.pallas_call(
+        own_kernel,
+        out_shape=pltpu.VMEM(shape, jnp.bfloat16),
+        in_specs=[pl.BlockSpec(memory_space=pltpu.SMEM), vmem, vmem],
+        out_specs=vmem,
+        scratch_shapes=[pltpu.VMEM(shape, jnp.float32)],
+        compiler_params=pltpu.CompilerParams(vmem_limit_bytes=8 * 2**20),
+    )(place, table, operands)
+
+
 def deposit_kernel(
     blocks, cycles, nphi, nyquist, place_ref, v_hbm, coords_hbm, t_hbm, o_hbm, table_hbm, wigner_hbm,
-    beam_hbm, own_ref, other_ref, wigner, beam, values, coords, cycle_of, pixels, fields, left, right, cube,
-    table, spread, sems,
+    beam_hbm, other_ref, operands, table, wigner, beam, values, coords, cycle_of, pixels, fields,
+    left, right, cube, spread, sems,
 ):
     sources = (v_hbm, coords_hbm, o_hbm, t_hbm, table_hbm, beam_hbm, wigner_hbm)
     targets = (values, coords, pixels, cycle_of, table, beam, wigner)
@@ -176,16 +219,10 @@
     runs = [jnp.concatenate(sums[b * per_run : (b + 1) * per_run], axis=1) for b in range(RADIX)]
     groups = phase_sums(runs)
     copies[4].wait()
-    half, share = own_ref.shape[0], own_ref.shape[1] // RADIX
-    count = table.shape[0] // RADIX
-    conjugate = jnp.where(
-        lax.broadcasted_iota(jnp.int32, (1, LANES), 1) < lines, 1.0, -1.0
-    )
-    start = 0
     for k, (real, imag) in enumerate(groups):
         real = split(real * (1.0 / math.sqrt(nphi)))
         imag = split(jnp.zeros_like(real[0], jnp.float32) if k == 0 else imag * (1.0 / math.sqrt(nphi)))
-        operand = jnp.concatenate(
+        operands[k] = jnp.concatenate(
             [
                 jnp.concatenate(pair, axis=1)
                 for r, i in zip(real, imag)
@@ -193,21 +230,7 @@
             ],
             axis=0,
         )
-        stop = start + count * len(members(k))
-        both = lax.dot_general(
-            table[start:stop].astype(jnp.bfloat16), operand, NT, preferred_element_type=jnp.float32
-        )
-        start = stop
-        both = both[:, :LANES] + both[:, LANES:]
-        for place, m in enumerate(members(k)):
-            waves = both[place * count : (place + 1) * count]
-            if place:
-                waves = waves * conjugate
-            for d in range(2 * half):
-                slot = d % 2 * half + d // 2
-                spread[slot, m * share : (m + 1) * share, :] = waves[d * share : (d + 1) * share]
-    own_ref[...] = spread[pl.ds(core * half, half)].astype(jnp.bfloat16)
-    other_ref[...] = spread[pl.ds((1 - core) * half, half)].astype(jnp.bfloat16)
+    transform(table.at[1 - core], operands, other_ref, spread)
     for copy in copies[5:]:
         copy.wait()
 
@@ -216,9 +239,9 @@
     orders, channels, cycles, waves = wigner.shape
     blocks = -(-nphi // STRIDE)
     rows = values.shape[0] // LANES
-    table = jnp.asarray(fourier_rows(nphi).astype(np.float32))
+    table = jnp.asarray(fourier_rows(nphi, tiles).astype(np.float32))
     vmem = pl.BlockSpec(memory_space=pltpu.VMEM)
-    whole = (tiles, orders, 2 * channels * cycles)
+    whole = (tiles // 2, orders, 2 * channels * cycles)
     wigner = wigner.reshape(orders * channels * cycles // BLOCK, BLOCK, waves)
     operands = (
         values.reshape(rows, LANES),
@@ -232,14 +255,15 @@
     return pl.pallas_call(
         lambda *refs: deposit_kernel(blocks, cycles, nphi, nyquist, *refs),
         out_shape=[
-            pltpu.VMEM((tiles // 2, *whole[1:]), jnp.bfloat16),
-            pltpu.VMEM((tiles // 2, *whole[1:]), jnp.bfloat16),
+            pltpu.VMEM(whole, jnp.bfloat16),
+            pltpu.VMEM((RADIX // 2 + 1, 2 * whole[2], 2 * BLOCK), jnp.bfloat16),
+            pltpu.VMEM(table.shape, jnp.float32),
             pltpu.VMEM(wigner.shape, wigner.dtype),
             pltpu.VMEM(beam.shape, beam.dtype),
         ],
         in_specs=[pl.BlockSpec(memory_space=pltpu.SMEM)]
         + [pl.BlockSpec(memory_space=pltpu.HBM)] * len(operands),
-        out_specs=[vmem] * 4,
+        out_specs=[vmem] * 5,
         scratch_shapes=[
             pltpu.VMEM((rows, LANES), jnp.float32),
             pltpu.VMEM(coords.shape, jnp.float32),
@@ -249,7 +273,6 @@
             pltpu.VMEM((channels * cycles * blocks, CHUNK), jnp.bfloat16),
             pltpu.VMEM((BLOCK, CHUNK), jnp.bfloat16),
             pltpu.VMEM((channels * cycles * blocks, BLOCK), jnp.float32),
-            pltpu.VMEM(table.shape, jnp.float32),
             pltpu.VMEM(whole, jnp.float32),
             pltpu.SemaphoreType.DMA((len(operands),)),
         ],
@@ -347,10 +370,11 @@
     nyquist = groups * channels // 2
     place = (2 * lax.axis_index("psi") + (lax.axis_index("theta") & 1)).astype(jnp.int32).reshape(1)
     samples = (sample_values, sample_coords, tile_ids, phi_pixels)
-    own, other, wigner, beam = partial_orders(
+    other, operands, table, wigner, beam = partial_orders(
         place, *samples, wigner_table, beam, nphi, nyquist, tiles
     )
     arrived = lax.ppermute(other, "theta", [(i, i ^ 1) for i in range(tiles)])
+    own = own_orders(place, table, operands, other.shape)
     freq = (own.astype(jnp.float32) + arrived.astype(jnp.float32)).astype(jnp.bfloat16)
     sides = [list(range(side, tiles, 2)) for side in range(2)]
     freq = lax.all_to_all(

time: 42.3 us -> 42.2 us (level)
  waiting for transfers between devices: 1.38 us -> 0.79 us
  Pallas kernels: 8.65 us -> 9.19 us
    ppermute x1, waiting for transfers between devices: 1.38 us -> 0.79 us  [body(): arrived = lax.ppermute(other, 'theta', [(i, i ^ 1) for i in range(tiles)])]
    pallas_call x0 -> x1, Pallas kernels: none -> 0.58 us  [own_orders(): pl.pallas_call(own_kernel, out_shape=pltpu.VMEM(shape, jnp.bfloat16), in_...]
  transfers between devices with their start and end apart: 1 -> 1, of which waited for: 1 -> 1; matrix products, arithmetic and copies ran while one was open for 0% -> 0% of each run, Pallas kernels for 0% -> 1%
where the time goes in v6:
time: 42.2 us; the launch traced here: 42.1 us
  blocking collectives  31.9 us (76%)
  Pallas kernels  9.19 us (22%)
  waiting for transfers between devices  0.79 us (2%)
    all_to_all x1, blocking collectives, body(): sky = lax.all_to_all(sky, 'psi', split_axis=0, concat_axis=0, tiled=True)  17.9 us
    all_to_all x1, blocking collectives, body(): lax.all_to_all(freq, 'theta', split_axis=0, concat_axis=0, axis_index_gro...  14.1 us
    pallas_call x1, Pallas kernels, partial_orders(): pl.pallas_call(lambda *refs: deposit_kernel(blocks, cycles, nphi, nyquist...  6.6 us
    pallas_call x1, Pallas kernels, partial_sky(): pl.pallas_call(lambda *refs: project_kernel(scale, *refs), out_shape=jax....  1.28 us
  transfers between devices with their start and end apart: 1, of which 1 were waited for; matrix products, arithmetic and copies ran while one was open for 0% of the time, Pallas kernels for 1%

profile of v6, /device:TPU:2, one launch (start us, length us, event | category | flops | bytes accessed | tf_op | source)
XLA Modules:
  0.0 42.1 jit_solution(3817653331773089740)
XLA Ops:
  0.0 6.6 %shard_map.73 = (bf16[16,36,128]{2,1,0:T(8,128)(2,1)S(1)}, bf16[5,256,512]{2,1,0:T(8,128)(2,1)S(1)}, f32[2,576,512]{2,1,0:T(8,128)S(1)}, bf16[9,256,1152]{2,1,0:T(8,128)(2,1)S(1)}, f32[2,1152]{1,0:T(2,128)S(1)}) custom-call(s32[1]{0:T(128)} %bitcast.refs_0_.place_ref, f32[64,128]{1,0:T(8,128)} %bitcast.7, f32[3,8192]{1,0:T(4,128)} %refs_2_.1, ...), custom_call_target="tpu_custom_call" | custom-call | tf_op jit(solution)/shard_map/pallas_call | solution.py:255
  6.6 0.1 collective-permute-start
  6.7 0.6 %shard_map.74 = bf16[16,36,128]{2,1,0:T(8,128)(2,1)S(1)} custom-call(s32[1]{0:T(128)} %bitcast.refs_0_.place_ref, f32[2,576,512]{2,1,0:T(8,128)S(1)} %get-tuple-element.10.table, bf16[5,256,512]{2,1,0:T(8,128)(2,1)S(1)} %get-tuple-element.11.operands), custom_call_target="tpu_custom_call" | custom-call | tf_op jit(solution)/shard_map/pallas_call | solution.py:108
  7.3 0.8 %collective-permute-done = bf16[16,36,128]{2,1,0:T(8,128)(2,1)S(1)} collective-permute-done((bf16[16,36,128]{2,1,0:T(8,128)(2,1)S(1)}, bf16[16,36,128]{2,1,0:T(8,128)(2,1)S(1)}, u32[]{:S(2)}, u32[]{:S(2)}) %collective-permute-start) | collective-permute-done | bytes 147488 | tf_op jit(solution)/shard_map/ppermute | solution.py:376
  8.1 14.1 %all_to_all.10.refs_0_ = bf16[16,36,128]{2,1,0:T(8,128)(2,1)S(1)} all-to-all(bf16[16,36,128]{2,1,0:T(8,128)(2,1)S(1)} %add_convert_fusion), channel_id=1, replica_groups={{0,2,4,6,8,10,12,14,16,18,20,22,24,26,28,30},{1,3,5,7,9,11,13,15,17,19,..., dimensions={0} | all-to-all | bytes 294912 | tf_op jit(solution)/shard_map/all_to_all | solution.py:380
  22.2 1.3 %shard_map.75 = bf16[8,81,128]{2,1,0:T(8,128)(2,1)S(1)} custom-call(bf16[16,36,128]{2,1,0:T(8,128)(2,1)S(1)} %all_to_all.10.refs_0_, bf16[9,256,1152]{2,1,0:T(8,128)(2,1)S(1)} %get-tuple-element.13.refs_1_, f32[2,1152]{1,0:T(2,128)S(1)} %get-tuple-element.14.refs_2_), custom_call_target="tpu_custom_call" | custom-call | tf_op jit(solution)/shard_map/pallas_call | solution.py:331
  23.5 17.9 %all_to_all.11.parts_ref = bf16[8,81,128]{2,1,0:T(8,128)(2,1)S(1)} all-to-all(bf16[8,81,128]{2,1,0:T(8,128)(2,1)S(1)} %shard_map.75), channel_id=1, replica_groups=mesh['psi'=8,'theta'=32] {'psi'}, dimensions={0} | all-to-all | bytes 331776 | tf_op jit(solution)/shard_map/all_to_all | solution.py:384
  41.4 0.7 %shard_map.76 = f32[36,2,144]{2,1,0:T(2,128)} custom-call(bf16[8,81,128]{2,1,0:T(8,128)(2,1)S(1)} %all_to_all.11.parts_ref), custom_call_target="tpu_custom_call" | custom-call | tf_op jit(solution)/shard_map/pallas_call | solution.py:356
  (1 shorter events, 0.0 us)
Async XLA Ops:
  6.6 1.5 %collective-permute-start = (bf16[16,36,128]{2,1,0:T(8,128)(2,1)S(1)}, bf16[16,36,128]{2,1,0:T(8,128)(2,1)S(1)}, u32[]{:S(2)}, u32[]{:S(2)}) collective-permute-start(bf16[16,36,128]{2,1,0:T(8,128)(2,1)S(1)} %get-tuple-element.12), channel_id=1, source_target_pairs={{0,1},{1,0},{2,3},{3,2},{4,5},{5,4},{6,7},{7,6},{8,9},{9,8},{10,11... | collective-permute-start | bytes 442376 | tf_op jit(solution)/shard_map/ppermute | solution.py:376
